TPU v7x, 32 devices: a whole 2x2x4 slice. The times are simulated.
32 devices in a mesh: ctx: 8 (over z, core), ch: 4 (over y, x).
Axes of the slice: x: 2, y: 2, z: 4, core: 2. Of those that a mesh axis runs over, the one named last changes fastest.
Arguments:
- query: bfloat16 [1024, 8192], P('ctx', 'ch'), may hold values from -6 to 6
- key: bfloat16 [1024, 8192], P('ctx', 'ch'), may hold values from -6 to 6
- value: bfloat16 [1024, 8192], P('ctx', 'ch'), may hold values from -6 to 6
- cotangent: bfloat16 [1024, 8192], P('ctx', 'ch'), may hold values from -6 to 6
- decay: float32 [4, 8192], P(None, 'ch'), may hold values from 0.95 to 1, as said below
- residue: float32 [4, 8192], P(None, 'ch'), may hold values from -3 to 3
- skip: float32 [8192], P('ch'), may hold values from -4 to 4
Outputs:
- output: bfloat16 [1024, 8192], P('ctx', 'ch')
- query_grad: bfloat16 [1024, 8192], P('ctx', 'ch')
- key_grad: bfloat16 [1024, 8192], P('ctx', 'ch')
- value_grad: bfloat16 [1024, 8192], P('ctx', 'ch')
- residue_grad: float32 [4, 8192], P(None, 'ch')
- skip_grad: float32 [8192], P('ch')
Inputs may be any that keep to these rules, and one draw needn't show every extreme that they name: decay lies below 1.
All inputs are finite; a program needn't handle non-finite values.
Results may differ from a plain program's by a relative error of at most 0.0012.
Values sent between devices are 32-bit elements; how exact they have to be, the bound alone decides.
A program may use at most 64 MiB of HBM per device.

v0:
```python
import math

import jax
import jax.numpy as jnp
from jax import lax
from jax.sharding import PartitionSpec as P

GROUP = 128


def local(query, key, value, cotangent, decay, residue, skip):
    tok_rows = query.shape[0]
    chan_width = query.shape[1]
    block_count = tok_rows // GROUP
    context = lax.axis_size("ctx")
    own_index = lax.axis_index("ctx")
    inner = key.astype(jnp.float32) * value.astype(jnp.float32)
    grad_z = cotangent.astype(jnp.float32) * query.astype(jnp.float32)
    log_decay = jnp.log(decay)
    spread = jnp.sqrt((1.0 - decay) * (1.0 + decay))
    coeffs = residue * spread
    position = jnp.arange(tok_rows, dtype=jnp.float32)
    tail_state = jnp.sum(
        jnp.exp((tok_rows - 1.0 - position)[None, :, None] * log_decay[:, None, :]) * inner[None],
        axis=1,
    )
    head_state = jnp.sum(
        jnp.exp(position[None, :, None] * log_decay[:, None, :]) * grad_z[None], axis=1
    )
    piece = (
        lax.all_gather(tail_state[None], "ctx", axis=0, tiled=True),
        lax.all_gather(head_state[None], "ctx", axis=0, tiled=True),
    )
    index = jnp.arange(piece[0].shape[0], dtype=jnp.int32)
    before = index < own_index
    after = index > own_index
    gap_before = jnp.where(before, own_index - 1 - index, 0).astype(jnp.float32)
    gap_after = jnp.where(after, index - own_index - 1, 0).astype(jnp.float32)
    weight_before = jnp.where(
        before[:, None, None], jnp.exp(gap_before[:, None, None] * tok_rows * log_decay[None]), 0.0
    )
    weight_after = jnp.where(
        after[:, None, None], jnp.exp(gap_after[:, None, None] * tok_rows * log_decay[None]), 0.0
    )
    carry_in = jnp.sum(weight_before * piece[0], axis=0)
    carry_back = jnp.sum(weight_after * piece[1], axis=0)
    steps_idx = jnp.arange(GROUP)
    lower = (steps_idx[:, None] >= steps_idx[None, :]).astype(jnp.float32)
    upper = lower.T

    def per_mode(totals, mode_data):
        mode_log, mode_coef, mode_in, mode_back = mode_data
        z_total, du_total = totals
        rising = jnp.exp(-position[:, None] * mode_log[None, :])
        falling = jnp.exp(position[:, None] * mode_log[None, :])
        scaled = (rising * inner).reshape(block_count, GROUP, chan_width)
        within = jnp.einsum("ts,bsc->btc", lower, scaled, precision=lax.Precision.HIGHEST)
        block_sums = jnp.sum(scaled, axis=1)
        earlier_sums = jnp.cumsum(block_sums, axis=0) - block_sums
        running = (within + earlier_sums[:, None, :]).reshape(tok_rows, chan_width)
        forward_state = falling * running + falling * jnp.exp(mode_log)[None, :] * mode_in[None, :]
        scaled_back = (falling * grad_z).reshape(block_count, GROUP, chan_width)
        within_back = jnp.einsum("ts,bsc->btc", upper, scaled_back, precision=lax.Precision.HIGHEST)
        back_sums = jnp.sum(scaled_back, axis=1)
        later_sums = jnp.sum(back_sums, axis=0)[None, :] - jnp.cumsum(back_sums, axis=0)
        running_back = (within_back + later_sums[:, None, :]).reshape(tok_rows, chan_width)
        backward_state = (
            rising * running_back
            + jnp.exp((tok_rows - position)[:, None] * mode_log[None, :]) * mode_back[None, :]
        )
        new_totals = (
            z_total + mode_coef[None, :] * forward_state,
            du_total + mode_coef[None, :] * backward_state,
        )
        return (new_totals, jnp.sum(grad_z * forward_state, axis=0))

    start_totals = (
        jnp.zeros((tok_rows, chan_width), jnp.float32),
        jnp.zeros((tok_rows, chan_width), jnp.float32),
    )
    (mixed, back_mixed), residue_terms = lax.scan(
        per_mode, start_totals, (log_decay, coeffs, carry_in, carry_back)
    )
    mixed_z = mixed + skip[None, :] * inner
    inner_grad = back_mixed + skip[None, :] * grad_z
    output = (query.astype(jnp.float32) * mixed_z).astype(jnp.bfloat16)
    query_grad = (cotangent.astype(jnp.float32) * mixed_z).astype(jnp.bfloat16)
    key_grad = (inner_grad * value.astype(jnp.float32)).astype(jnp.bfloat16)
    value_grad = (inner_grad * key.astype(jnp.float32)).astype(jnp.bfloat16)
    residue_local = spread * residue_terms
    skip_local = jnp.sum(grad_z * inner, axis=0)
    residue_sum, skip_sum = lax.psum((residue_local, skip_local), "ctx")
    scale = 1.0 / math.sqrt(tok_rows * context)
    return (output, query_grad, key_grad, value_grad, residue_sum * scale, skip_sum * scale)


def solution(mesh):
    in_specs = (
        P("ctx", "ch"),
        P("ctx", "ch"),
        P("ctx", "ch"),
        P("ctx", "ch"),
        P(None, "ch"),
        P(None, "ch"),
        P("ch"),
    )
    out_specs = (
        P("ctx", "ch"),
        P("ctx", "ch"),
        P("ctx", "ch"),
        P("ctx", "ch"),
        P(None, "ch"),
        P("ch"),
    )
    return jax.shard_map(local, mesh=mesh, in_specs=in_specs, out_specs=out_specs, check_vma=False)
```

profile of v0, /device:TPU:0, one launch (start us, length us, event | category | flops | bytes accessed | tf_op | source)
XLA Modules:
  0.0 105.8 jit_solution(9496550172265131183)
XLA Ops:
  0.7 0.8 fusion.39
  1.5 1.8 %convert_multiply_fusion.1 = (f32[128,2048]{1,0:T(8,128)S(1)}, f32[128,2048]{1,0:T(8,128)S(1)}) fusion(bf16[128,2048]{1,0:T(8,128)(2,1)} %param.12, bf16[128,2048]{1,0:T(8,128)(2,1)} %param.9, bf16[128,2048]{1,0:T(8,128)(2,1)} %param.11, bf16[128,2048]{1,0:T(8,128)(2,1)} %param.10), kind=kLoop, calls=%fused_computation.43 | loop fusion | flops 1572864 | bytes 4194304 | tf_op jit(solution)/shard_map/mul | solution.py:18
  3.4 0.0 copy-start.4
  3.4 1.5 %multiply_reduce_fusion.1 = (f32[4,2048]{1,0:T(4,128)S(1)}, f32[4,2048]{1,0:T(4,128)S(1)}) fusion(f32[128,2048]{1,0:T(8,128)S(1)} %get-tuple-element.345, f32[4,2048]{1,0:T(4,128)S(1)} %get-tuple-element.342, f32[128,2048]{1,0:T(8,128)S(1)} %get-tuple-element.343, f32[128]{0:T(128)S(1)} %iota_subtract_fusion.1), kind=kLoop, calls=%fused_computation.40 | loop fusion | flops 6275072 | bytes 2195968 | tf_op jit(solution)/shard_map/reduce_sum | solution.py:27
  4.9 0.0 copy-done.4
  4.9 15.9 %all-gather.2 = f32[8,4,2048]{2,1,0:T(4,128)S(1)} all-gather(f32[1,4,2048]{2,1,0:T(4,128)S(1)} %bitcast.82), channel_id=2, replica_groups=mesh['ctx'=8,'ch'=4] {'ctx'}, dimensions={0}, use_global_device_ids=true | all-gather | bytes 294912 | tf_op jit(solution)/shard_map/all_gather | solution.py:31
  20.8 14.2 %all-gather.3 = f32[8,4,2048]{2,1,0:T(4,128)S(1)} all-gather(f32[1,4,2048]{2,1,0:T(4,128)S(1)} %bitcast.81), channel_id=3, replica_groups=mesh['ctx'=8,'ch'=4] {'ctx'}, dimensions={0}, use_global_device_ids=true | all-gather | bytes 294912 | tf_op jit(solution)/shard_map/all_gather | solution.py:32
  34.9 0.4 multiply_reduce_fusion.4
  35.4 0.0 copy-start.5
  35.4 0.0 copy-start
  35.4 0.0 copy-start.1
  35.4 0.0 copy-start.2
  35.4 0.0 copy-start.3
  35.4 0.0 copy-start.6
  35.4 35.6 %while.17 = (s32[]{:T(128)}, f32[128,2048]{1,0:T(8,128)}, f32[128,2048]{1,0:T(8,128)}, f32[4,2048]{1,0:T(4,128)S(1)}, f32[4,2048]{1,0:T(4,128)S(1)}, /*index=5*/...) while((s32[]{:T(128)}, f32[128,2048]{1,0:T(8,128)}, ...), condition=%wide.region_8.9_spmd.clone.clone, body=%wide.region_4.8_spmd.clone.clone.sunk | while | flops 812972288 | bytes 8637588 | solution.py:81
  35.5 0.3 fusion.48
  35.8 4.3 %multiply_reduce_fusion.7 = (f32[2048]{0:T(1024)S(1)}, f32[2048]{0:T(1024)S(1)}, f32[128,2048]{1,0:T(8,128)}) fusion(f32[128,2048]{1,0:T(8,128)} %get-tuple-element.369, f32[2048]{0:T(1024)S(1)} %bitcast.73, f32[2048]{0:T(1024)S(1)} %bitcast.77, f32[128,2048]{1,0:T(8,128)} %get-tuple-element.350, pred[]{:T(512)S(6)} %compare.3, ...), kind=kOutput, calls=%fused_computation.22.clone.1 | convolution fusion | flops 406614016 | bytes 4252161 | tf_op jit(solution)/shard_map/while/body/eval_jaxpr/ts,bsc->btc/dot_general | solution.py:57
  40.1 0.1 dynamic_update_slice.8
  40.2 3.8 %fusion.49 = f32[128,2048]{1,0:T(8,128)} fusion(f32[128,2048]{1,0:T(8,128)} %get-tuple-element.351, f32[128,2048]{1,0:T(8,128)} %get-tuple-element.369, f32[2048]{0:T(1024)S(1)} %bitcast.76, f32[128]{0:T(128)S(1)} %iota_subtract_fusion.3, f32[2048]{0:T(1024)S(1)} %sub.96, f32[128]{0:T(128)S(1)} %negate_bitcast_fusion.2, f32[2048]{0:T(1024)S(1)} %bitcast.74, ...), kind=kOutput, calls=%fused_computation.13.clone.1 | convolution fusion | flops 405569536 | bytes 3179521 | tf_op jit(solution)/shard_map/while/body/eval_jaxpr/ts,bsc->btc/dot_general | solution.py:63
  44.1 0.3 fusion.48
  44.4 4.4 %multiply_reduce_fusion.7 = (f32[2048]{0:T(1024)S(1)}, f32[2048]{0:T(1024)S(1)}, f32[128,2048]{1,0:T(8,128)}) fusion(f32[128,2048]{1,0:T(8,128)} %get-tuple-element.369, f32[2048]{0:T(1024)S(1)} %bitcast.73, f32[2048]{0:T(1024)S(1)} %bitcast.77, f32[128,2048]{1,0:T(8,128)} %get-tuple-element.350, pred[]{:T(512)S(6)} %compare.3, ...), kind=kOutput, calls=%fused_computation.22.clone.1 | convolution fusion | flops 406614016 | bytes 4252161 | tf_op jit(solution)/shard_map/while/body/eval_jaxpr/ts,bsc->btc/dot_general | solution.py:57
  48.8 0.1 dynamic_update_slice.8
  48.9 4.2 %fusion.49 = f32[128,2048]{1,0:T(8,128)} fusion(f32[128,2048]{1,0:T(8,128)} %get-tuple-element.351, f32[128,2048]{1,0:T(8,128)} %get-tuple-element.369, f32[2048]{0:T(1024)S(1)} %bitcast.76, f32[128]{0:T(128)S(1)} %iota_subtract_fusion.3, f32[2048]{0:T(1024)S(1)} %sub.96, f32[128]{0:T(128)S(1)} %negate_bitcast_fusion.2, f32[2048]{0:T(1024)S(1)} %bitcast.74, ...), kind=kOutput, calls=%fused_computation.13.clone.1 | convolution fusion | flops 405569536 | bytes 3179521 | tf_op jit(solution)/shard_map/while/body/eval_jaxpr/ts,bsc->btc/dot_general | solution.py:63
  53.1 0.3 fusion.48
  53.4 4.4 %multiply_reduce_fusion.7 = (f32[2048]{0:T(1024)S(1)}, f32[2048]{0:T(1024)S(1)}, f32[128,2048]{1,0:T(8,128)}) fusion(f32[128,2048]{1,0:T(8,128)} %get-tuple-element.369, f32[2048]{0:T(1024)S(1)} %bitcast.73, f32[2048]{0:T(1024)S(1)} %bitcast.77, f32[128,2048]{1,0:T(8,128)} %get-tuple-element.350, pred[]{:T(512)S(6)} %compare.3, ...), kind=kOutput, calls=%fused_computation.22.clone.1 | convolution fusion | flops 406614016 | bytes 4252161 | tf_op jit(solution)/shard_map/while/body/eval_jaxpr/ts,bsc->btc/dot_general | solution.py:57
  57.8 0.1 dynamic_update_slice.8
  57.9 4.2 %fusion.49 = f32[128,2048]{1,0:T(8,128)} fusion(f32[128,2048]{1,0:T(8,128)} %get-tuple-element.351, f32[128,2048]{1,0:T(8,128)} %get-tuple-element.369, f32[2048]{0:T(1024)S(1)} %bitcast.76, f32[128]{0:T(128)S(1)} %iota_subtract_fusion.3, f32[2048]{0:T(1024)S(1)} %sub.96, f32[128]{0:T(128)S(1)} %negate_bitcast_fusion.2, f32[2048]{0:T(1024)S(1)} %bitcast.74, ...), kind=kOutput, calls=%fused_computation.13.clone.1 | convolution fusion | flops 405569536 | bytes 3179521 | tf_op jit(solution)/shard_map/while/body/eval_jaxpr/ts,bsc->btc/dot_general | solution.py:63
  62.1 0.3 fusion.48
  62.4 4.4 %multiply_reduce_fusion.7 = (f32[2048]{0:T(1024)S(1)}, f32[2048]{0:T(1024)S(1)}, f32[128,2048]{1,0:T(8,128)}) fusion(f32[128,2048]{1,0:T(8,128)} %get-tuple-element.369, f32[2048]{0:T(1024)S(1)} %bitcast.73, f32[2048]{0:T(1024)S(1)} %bitcast.77, f32[128,2048]{1,0:T(8,128)} %get-tuple-element.350, pred[]{:T(512)S(6)} %compare.3, ...), kind=kOutput, calls=%fused_computation.22.clone.1 | convolution fusion | flops 406614016 | bytes 4252161 | tf_op jit(solution)/shard_map/while/body/eval_jaxpr/ts,bsc->btc/dot_general | solution.py:57
  66.8 0.1 dynamic_update_slice.8
  66.9 4.2 %fusion.49 = f32[128,2048]{1,0:T(8,128)} fusion(f32[128,2048]{1,0:T(8,128)} %get-tuple-element.351, f32[128,2048]{1,0:T(8,128)} %get-tuple-element.369, f32[2048]{0:T(1024)S(1)} %bitcast.76, f32[128]{0:T(128)S(1)} %iota_subtract_fusion.3, f32[2048]{0:T(1024)S(1)} %sub.96, f32[128]{0:T(128)S(1)} %negate_bitcast_fusion.2, f32[2048]{0:T(1024)S(1)} %bitcast.74, ...), kind=kOutput, calls=%fused_computation.13.clone.1 | convolution fusion | flops 405569536 | bytes 3179521 | tf_op jit(solution)/shard_map/while/body/eval_jaxpr/ts,bsc->btc/dot_general | solution.py:63
  71.0 0.0 copy-done.5
  71.1 0.0 copy-done
  71.1 0.0 copy-done.1
  71.1 0.0 copy-done.2
  71.1 0.0 copy-done.3
  71.1 0.0 copy-done.6
  71.1 3.9 %fusion.35 = (bf16[128,2048]{1,0:T(8,128)(2,1)}, bf16[128,2048]{1,0:T(8,128)(2,1)}, bf16[128,2048]{1,0:T(8,128)(2,1)}, bf16[128,2048]{1,0:T(8,128)(2,1)}, f32[2048]{0:T(1024)S(1)}) fusion(bf16[128,2048]{1,0:T(8,128)(2,1)S(1)} %copy-done, f32[128,2048]{1,0:T(8,128)} %get-tuple-element.135, f32[2048]{0:T(1024)S(1)} %copy-done.6, ...), kind=kLoop, calls=%fused_computation.51 | loop fusion | flops 5240832 | bytes 6307840 | tf_op jit(solution)/shard_map/convert_element_type | solution.py:87
  75.0 29.6 %all-reduce = (f32[4,2048]{1,0:T(4,128)S(1)}, f32[2048]{0:T(1024)S(1)}) all-reduce(f32[4,2048]{1,0:T(4,128)S(1)} %fusion.36, f32[2048]{0:T(1024)S(1)} %get-tuple-element.251), channel_id=1, replica_groups=mesh['ctx'=8,'ch'=4] {'ctx'}, use_global_device_ids=true, to_apply=%region_9.10 | all-reduce | flops 10240 | bytes 81920 | tf_op jit(solution)/shard_map/psum | solution.py:92
  104.6 0.6 broadcast_multiply_fusion
  105.2 0.6 broadcast_multiply_fusion.1
  (31 shorter events, 0.3 us)
Async XLA Ops:
  3.4 1.5 %copy-start.4 = (f32[128,2048]{1,0:T(8,128)}, f32[128,2048]{1,0:T(8,128)S(1)}, u32[]{:S(2)}) copy-start(f32[128,2048]{1,0:T(8,128)S(1)} %get-tuple-element.345) | copy-start | bytes 3145732
  35.4 35.7 %copy-start.5 = (f32[4,2048]{1,0:T(4,128)S(1)}, f32[4,2048]{1,0:T(4,128)}, u32[]{:S(2)}) copy-start(f32[4,2048]{1,0:T(4,128)} %param.13) | copy-start | bytes 98308
  35.4 35.7 %copy-start = (bf16[128,2048]{1,0:T(8,128)(2,1)S(1)}, bf16[128,2048]{1,0:T(8,128)(2,1)}, u32[]{:S(2)}) copy-start(bf16[128,2048]{1,0:T(8,128)(2,1)} %param.12) | copy-start | bytes 1572868
  35.4 35.7 %copy-start.1 = (bf16[128,2048]{1,0:T(8,128)(2,1)S(1)}, bf16[128,2048]{1,0:T(8,128)(2,1)}, u32[]{:S(2)}) copy-start(bf16[128,2048]{1,0:T(8,128)(2,1)} %param.9) | copy-start | bytes 1572868
  35.4 35.7 %copy-start.2 = (bf16[128,2048]{1,0:T(8,128)(2,1)S(1)}, bf16[128,2048]{1,0:T(8,128)(2,1)}, u32[]{:S(2)}) copy-start(bf16[128,2048]{1,0:T(8,128)(2,1)} %param.11) | copy-start | bytes 1572868
  35.4 35.7 %copy-start.3 = (bf16[128,2048]{1,0:T(8,128)(2,1)S(1)}, bf16[128,2048]{1,0:T(8,128)(2,1)}, u32[]{:S(2)}) copy-start(bf16[128,2048]{1,0:T(8,128)(2,1)} %param.10) | copy-start | bytes 1572868
  35.4 35.7 %copy-start.6 = (f32[2048]{0:T(1024)S(1)}, f32[2048]{0:T(1024)}, u32[]{:S(2)}) copy-start(f32[2048]{0:T(1024)} %param.15) | copy-start | bytes 24580
where the time goes:
time: 106 us
  blocking collectives  59.6 us (56%)
  matrix products  33.7 us (32%)
  other arithmetic  10.9 us (10%)
    psum x1, blocking collectives, local(): residue_sum, skip_sum = lax.psum((residue_local, skip_local), 'ctx')  29.6 us
    dot_general x4, matrix products, per_mode(): jnp.einsum('ts,bsc->btc', lower, scaled, precision=lax.Precision.HIGHEST)  17.4 us
    dot_general x4, matrix products, per_mode(): jnp.einsum('ts,bsc->btc', upper, scaled_back, precision=lax.Precision.HIG...  16.3 us
    all_gather x1, blocking collectives, local(): lax.all_gather(tail_state[None], 'ctx', axis=0, tiled=True)  15.9 us
    all_gather x1, blocking collectives, local(): lax.all_gather(head_state[None], 'ctx', axis=0, tiled=True)  14.2 us
    convert_element_type x1, other arithmetic, local(): query_grad = (cotangent.astype(jnp.float32) * mixed_z).astype(jnp.bfloat16)  3.92 us

commit v1 on v0

v1 whole, which is shorter than its diff:
```python
import functools
import math

import jax
import jax.numpy as jnp
from jax import lax
from jax.experimental import pallas as pl
from jax.experimental.pallas import tpu as pltpu
from jax.sharding import PartitionSpec as P

LANES = 128
SEGS = 8
F32 = jnp.float32
MESH = pl.DeviceIdType.MESH


def each(low, high, body):
    if high - low <= 16:
        for step in range(low, high):
            body(step)
    else:
        def wrapped(step, carry):
            body(step)
            return carry

        lax.fori_loop(low, high, wrapped, 0)


def power(base, exponent):
    result = None
    while exponent:
        if exponent & 1:
            result = base if result is None else result * base
        exponent >>= 1
        if exponent:
            base = base * base
    return result


def kernel(
    n, m, scale,
    q_hbm, k_hbm, v_hbm, g_hbm, decay_hbm, residue_hbm, skip_hbm,
    out_hbm, dq_hbm, dk_hbm, dv_hbm, res_ref, skipg_ref,
    q_in, k_in, v_in, g_in, decay, residue, skip, coef,
    out_v, dq_v, dk_v, dv_v,
    x_s, z_s, y_s, u_s, seg, start,
    mine, gath, ret, carry, rsend, rgath, rtot,
    in_sem, par_sem, out_sem, s1s, s1r, s2s, s2r, s3s, s3r, s4s, s4r,
):
    me = lax.axis_index("ctx")
    rows = q_hbm.shape[0]
    width = q_hbm.shape[1] // m
    tiles = width // LANES
    modes = decay_hbm.shape[0]
    steps = rows // SEGS
    stride = n // m
    own = me // stride
    hbm_in = (q_hbm, k_hbm, v_hbm, g_hbm)
    vmem_in = (q_in, k_in, v_in, g_in)
    hbm_out = (out_hbm, dq_hbm, dk_hbm, dv_hbm)
    vmem_out = (out_v, dq_v, dk_v, dv_v)

    def block_of(step):
        return lax.rem(me + 1 + step, m)

    def lanes_of(block, tile=None):
        if tile is None:
            return pl.ds(pl.multiple_of(block * width, LANES), width)
        return pl.ds(pl.multiple_of(block * width + tile * LANES, LANES), LANES)

    def load_copy(index, block):
        return pltpu.make_async_copy(
            hbm_in[index].at[:, lanes_of(block)], vmem_in[index].at[block],
            in_sem.at[index, block],
        )

    def store_copy(index, block):
        return pltpu.make_async_copy(
            vmem_out[index].at[block], hbm_out[index].at[:, lanes_of(block)],
            out_sem.at[index, block],
        )

    params = [
        pltpu.make_async_copy(decay_hbm, decay, par_sem.at[0]),
        pltpu.make_async_copy(residue_hbm, residue, par_sem.at[1]),
        pltpu.make_async_copy(skip_hbm, skip, par_sem.at[2]),
    ]

    def remote(src, dst, send_sem, recv_sem, device):
        return pltpu.make_async_remote_copy(
            src_ref=src, dst_ref=dst, send_sem=send_sem, recv_sem=recv_sem,
            device_id={"ctx": device}, device_id_type=MESH,
        )

    def ends_copy(block):
        return remote(mine.at[block], gath.at[me], s1s.at[block], s1r.at[me], block * stride)

    def return_copy(peer):
        return remote(ret.at[peer], carry.at[own], s2s.at[peer], s2r.at[own], peer)

    def sums_copy(block):
        return remote(rsend.at[block], rgath.at[me], s3s.at[block], s3r.at[me], block * stride)

    def total_copy(peer):
        return remote(rtot.at[own], rtot.at[own], s4s.at[peer], s4r.at[own], peer)

    def as_owner(body):
        if stride == 1:
            body()
        else:
            pl.when(lax.rem(me, stride) == 0)(body)

    def peers(body):
        each(1, n, lambda r: body(lax.rem(me + r, n)))

    def row(ref, mode, block, tile):
        return jnp.broadcast_to(ref[mode:mode + 1, lanes_of(block, tile)], (SEGS, LANES))

    def strided(index):
        return pl.ds(index, SEGS, stride=steps)

    barrier = pltpu.get_barrier_semaphore()
    for copy in params:
        copy.start()
    for step in range(m):
        for index in range(4):
            load_copy(index, block_of(step)).start()
    peers(lambda peer: pl.semaphore_signal(
        barrier, inc=1, device_id={"ctx": peer}, device_id_type=MESH))
    for copy in params:
        copy.wait()

    def first_pass(block):
        for index in range(4):
            load_copy(index, block).wait()
        for tile in range(tiles):
            spot = block * tiles + tile
            here = slice(tile * LANES, (tile + 1) * LANES)
            x_s[spot] = k_in[block, :, here].astype(F32) * v_in[block, :, here].astype(F32)
            z_s[spot] = g_in[block, :, here].astype(F32) * q_in[block, :, here].astype(F32)
            d_all = decay[:, lanes_of(block, tile)]
            spread = jnp.sqrt((1.0 - d_all) * (1.0 + d_all))
            coef[:, lanes_of(block, tile)] = residue[:, lanes_of(block, tile)] * spread
            d = [row(decay, mode, block, tile) for mode in range(modes)]
            tail = [None] * modes
            head = [None] * modes
            for i in range(steps):
                x = x_s[spot, strided(i), :]
                z = z_s[spot, strided(steps - 1 - i), :]
                for mode in range(modes):
                    tail[mode] = x if i == 0 else d[mode] * tail[mode] + x
                    head[mode] = z if i == 0 else d[mode] * head[mode] + z
            for mode in range(modes):
                seg[tile, mode * SEGS:(mode + 1) * SEGS, :] = tail[mode]
                seg[tile, (modes + mode) * SEGS:(modes + mode + 1) * SEGS, :] = head[mode]
            d_seg = power(d_all, steps)
            total = jnp.zeros((modes, LANES), F32)
            for j in range(SEGS):
                at = pl.ds(j, modes, stride=SEGS)
                start[spot, at, :] = total
                total = d_seg * total + seg[tile, at, :]
            mine[block, 0:modes, here] = total
            total = jnp.zeros((modes, LANES), F32)
            for j in reversed(range(SEGS)):
                at = pl.ds(modes * SEGS + j, modes, stride=SEGS)
                start[spot, at, :] = total
                total = d_seg * total + seg[tile, at, :]
            mine[block, modes:2 * modes, here] = total

    def send_ends(block):
        @pl.when(block * stride != me)
        def _():
            ends_copy(block).start()

        @pl.when(block * stride == me)
        def _():
            gath[me] = mine[block]

    def middle_pass(block):
        for tile in range(tiles):
            spot = block * tiles + tile
            here = slice(tile * LANES, (tile + 1) * LANES)
            d = [row(decay, mode, block, tile) for mode in range(modes)]
            c = [row(coef, mode, block, tile) for mode in range(modes)]
            sk = row(skip, 0, block, tile)
            state = [start[spot, mode * SEGS:(mode + 1) * SEGS, :] for mode in range(modes)]
            back = [
                start[spot, (modes + mode) * SEGS:(modes + mode + 1) * SEGS, :]
                for mode in range(modes)
            ]
            sums = [jnp.zeros((SEGS, LANES), F32) for _ in range(modes + 1)]
            for i in range(steps):
                x = x_s[spot, strided(i), :]
                z = z_s[spot, strided(i), :]
                y = sk * x
                sums[modes] = sums[modes] + z * x
                for mode in range(modes):
                    state[mode] = d[mode] * state[mode] + x
                    y = y + c[mode] * state[mode]
                    sums[mode] = sums[mode] + z * state[mode]
                y_s[spot, strided(i), :] = y
                z = z_s[spot, strided(steps - 1 - i), :]
                u = sk * z
                for mode in range(modes):
                    back[mode] = d[mode] * back[mode] + z
                    u = u + c[mode] * back[mode]
                u_s[spot, strided(steps - 1 - i), :] = u
            for mode in range(modes + 1):
                rsend[block, mode:mode + 1, here] = jnp.sum(sums[mode], axis=0, keepdims=True)
            rsend[block, modes + 1:, here] = jnp.zeros((2 * modes - modes - 1, LANES), F32)

    def send_sums(block):
        @pl.when(block * stride != me)
        def _():
            sums_copy(block).start()

        @pl.when(block * stride == me)
        def _():
            rgath[me] = rsend[block]

    def owner_scan():
        peers(lambda peer: remote(
            gath.at[peer], gath.at[peer], s1s.at[0], s1r.at[peer], peer).wait_recv())
        d_rows = power(decay[:, lanes_of(own)], rows)

        def forward(p, total):
            ret[p, 0:modes, :] = total
            return d_rows * total + gath[p, 0:modes, :]

        def backward(p, total):
            ret[n - 1 - p, modes:2 * modes, :] = total
            return d_rows * total + gath[n - 1 - p, modes:2 * modes, :]

        zero = jnp.zeros((modes, width), F32)
        lax.fori_loop(0, n, forward, zero, unroll=n <= 16)
        lax.fori_loop(0, n, backward, zero, unroll=n <= 16)
        carry[own] = ret[me]
        peers(lambda peer: return_copy(peer).start())

    def owner_sums():
        peers(lambda peer: remote(
            rgath.at[peer], rgath.at[peer], s3s.at[0], s3r.at[peer], peer).wait_recv())

        def add(p, total):
            return (
                total[0] + rgath[p],
                total[1] + gath[p, modes:2 * modes, :] * ret[p, 0:modes, :],
            )

        whole, cross = lax.fori_loop(
            0, n, add,
            (jnp.zeros((2 * modes, width), F32), jnp.zeros((modes, width), F32)),
            unroll=n <= 16,
        )
        d_all = decay[:, lanes_of(own)]
        spread = jnp.sqrt((1.0 - d_all) * (1.0 + d_all))
        rtot[own, 0:modes, :] = (whole[0:modes] + d_all * cross) * (spread * scale)
        rtot[own, modes:2 * modes, :] = whole[modes:2 * modes] * scale
        peers(lambda peer: total_copy(peer).start())

    place = lax.broadcasted_iota(jnp.int32, (SEGS, LANES), 0)
    bits = [(place & (1 << bit)) != 0 for bit in range(3)]

    def last_pass(block):
        for tile in range(tiles):
            spot = block * tiles + tile
            here = slice(tile * LANES, (tile + 1) * LANES)
            fall = []
            fore = []
            aft = []
            for mode in range(modes):
                base = row(decay, mode, block, tile)
                weight = row(coef, mode, block, tile) * base
                up = weight * jnp.broadcast_to(carry[block, mode:mode + 1, here], (SEGS, LANES))
                down = weight * jnp.broadcast_to(
                    carry[block, modes + mode:modes + mode + 1, here], (SEGS, LANES))
                for bit in bits:
                    up = jnp.where(bit, up * base, up)
                    down = jnp.where(bit, down, down * base)
                    base = base * base
                fall.append(base)
                fore.append(up)
                aft.append(down)
            for pair in range(rows // 16):
                parts = []
                for half in range(2):
                    at = slice(pair * 16 + half * 8, pair * 16 + half * 8 + 8)
                    parts.append(y_s[spot, at, :] + ((fore[0] + fore[1]) + (fore[2] + fore[3])))
                    fore = [value * rate for value, rate in zip(fore, fall)]
                mixed = jnp.concatenate(parts, axis=0)
                at = slice(pair * 16, pair * 16 + 16)
                out_v[block, at, here] = (q_in[block, at, here].astype(F32) * mixed).astype(jnp.bfloat16)
                dq_v[block, at, here] = (g_in[block, at, here].astype(F32) * mixed).astype(jnp.bfloat16)
                pair = rows // 16 - 1 - pair
                parts = []
                for half in (1, 0):
                    at = slice(pair * 16 + half * 8, pair * 16 + half * 8 + 8)
                    parts.append(u_s[spot, at, :] + ((aft[0] + aft[1]) + (aft[2] + aft[3])))
                    aft = [value * rate for value, rate in zip(aft, fall)]
                mixed = jnp.concatenate(parts[::-1], axis=0)
                at = slice(pair * 16, pair * 16 + 16)
                dk_v[block, at, here] = (v_in[block, at, here].astype(F32) * mixed).astype(jnp.bfloat16)
                dv_v[block, at, here] = (k_in[block, at, here].astype(F32) * mixed).astype(jnp.bfloat16)

    first_pass(block_of(0))
    pl.semaphore_wait(barrier, n - 1)
    send_ends(block_of(0))

    @pl.loop(1, m)
    def _(step):
        block = block_of(step)
        first_pass(block)
        send_ends(block)

    half = m // 2

    def middle(step):
        block = block_of(step)
        middle_pass(block)
        send_sums(block)

    pl.loop(0, half)(middle)
    as_owner(owner_scan)
    pl.loop(half, m)(middle)

    def last(step):
        block = block_of(m - 1 + step)

        @pl.when(block * stride != me)
        def _():
            remote(carry.at[block], carry.at[block], s2s.at[0], s2r.at[block], me).wait_recv()

        last_pass(block)
        for index in range(4):
            store_copy(index, block).start()

    pl.loop(0, half)(last)
    as_owner(owner_sums)
    pl.loop(half, m)(last)

    for block in range(m):
        @pl.when(block * stride != me)
        def _():
            remote(rtot.at[block], rtot.at[block], s4s.at[0], s4r.at[block], me).wait_recv()
            ends_copy(block).wait_send()
            sums_copy(block).wait_send()

        at = slice(block * width, (block + 1) * width)
        res_ref[:, at] = rtot[block, 0:modes, :]
        skipg_ref[:, at] = rtot[block, modes:modes + 1, :]

    def sent():
        def one(peer):
            return_copy(peer).wait_send()
            total_copy(peer).wait_send()

        peers(one)

    as_owner(sent)

    @pl.loop(0, m)
    def _(block):
        for index in range(4):
            store_copy(index, block).wait()


def local(n, query, key, value, cotangent, decay, residue, skip):
    rows, chans = query.shape
    modes = decay.shape[0]
    m = min(n, chans // LANES)
    width = chans // m
    scale = 1.0 / math.sqrt(rows * n)
    wide = jax.ShapeDtypeStruct((rows, chans), jnp.bfloat16)
    anywhere = pl.BlockSpec(memory_space=pl.ANY)
    vmem = pl.BlockSpec(memory_space=pltpu.VMEM)
    blocks16 = pltpu.VMEM((m, rows, width), jnp.bfloat16)
    plane = pltpu.VMEM((chans // LANES, rows, LANES), F32)
    by_owner = pltpu.VMEM((m, 2 * modes, width), F32)
    by_device = pltpu.VMEM((n, 2 * modes, width), F32)
    dma = pltpu.SemaphoreType.DMA
    outs = pl.pallas_call(
        functools.partial(kernel, n, m, scale),
        out_shape=(
            wide, wide, wide, wide,
            jax.ShapeDtypeStruct((modes, chans), F32),
            jax.ShapeDtypeStruct((1, chans), F32),
        ),
        in_specs=[anywhere] * 7,
        out_specs=(anywhere,) * 4 + (vmem,) * 2,
        scratch_shapes=[
            blocks16, blocks16, blocks16, blocks16,
            pltpu.VMEM((modes, chans), F32),
            pltpu.VMEM((modes, chans), F32),
            pltpu.VMEM((1, chans), F32),
            pltpu.VMEM((modes, chans), F32),
            blocks16, blocks16, blocks16, blocks16,
            plane, plane, plane, plane,
            pltpu.VMEM((width // LANES, 2 * modes * SEGS, LANES), F32),
            pltpu.VMEM((chans // LANES, 2 * modes * SEGS, LANES), F32),
            by_owner, by_device, by_device, by_owner, by_owner, by_device, by_owner,
            dma((4, m)), dma((3,)), dma((4, m)),
            dma((m,)), dma((n,)), dma((n,)), dma((m,)),
            dma((m,)), dma((n,)), dma((n,)), dma((m,)),
        ],
        compiler_params=pltpu.CompilerParams(
            collective_id=0, has_side_effects=True, vmem_limit_bytes=20 * 1024 * 1024,
        ),
        cost_estimate=pl.CostEstimate(
            flops=80 * rows * chans, bytes_accessed=16 * rows * chans, transcendentals=0
        ),
        name="hyena",
    )(query, key, value, cotangent, decay, residue, skip.reshape(1, chans))
    return outs[:5] + (outs[5].reshape(chans),)


def solution(mesh):
    wide = P("ctx", "ch")
    thin = P(None, "ch")
    return jax.shard_map(
        functools.partial(local, mesh.shape["ctx"]),
        mesh=mesh,
        in_specs=(wide, wide, wide, wide, thin, thin, P("ch")),
        out_specs=(wide, wide, wide, wide, thin, P("ch")),
        check_vma=False,
    )
```

time: 106 us -> 30.4 us (0.29)
  blocking collectives: 59.6 us -> 0 us
  matrix products: 33.7 us -> 0 us
  Pallas kernels: 0 us -> 18.5 us
  other arithmetic: 10.9 us -> 0 us
  local copies, waits for them, and re-layouts: 0.64 us -> 10.8 us
    dot_general x8 -> x0, matrix products: 33.7 us -> none  [the longest x4 17.4 us: per_mode(): jnp.einsum('ts,bsc->btc', lower, scaled, precision=lax.Precision.HIGHEST)]
    all_gather x2 -> x0, blocking collectives: 30.1 us -> none  [the longest x1 15.9 us: local(): lax.all_gather(tail_state[None], 'ctx', axis=0, tiled=True)]
    psum x1 -> x0, blocking collectives: 29.6 us -> none  [local(): residue_sum, skip_sum = lax.psum((residue_local, skip_local), 'ctx')]
    pallas_call x0 -> x1, Pallas kernels: none -> 18.5 us  [local(): pl.pallas_call(functools.partial(kernel, n, m, scale), out_shape=(wide, w...]
    unnamed x14 -> x20, local copies, waits for them, and re-layouts: 0.04 us -> 10.8 us
    convert_element_type x1 -> x0, other arithmetic: 3.92 us -> none  [local(): query_grad = (cotangent.astype(jnp.float32) * mixed_z).astype(jnp.bfloat16)]
    mul x9 -> x0, other arithmetic: 3.14 us -> none  [the longest x1 1.84 us: local(): grad_z = cotangent.astype(jnp.float32) * query.astype(jnp.float32)]
    reduce_sum x6 -> x0, other arithmetic: 2.92 us -> none  [the longest x1 1.49 us: local(): jnp.sum(jnp.exp(position[None, :, None] * log_decay[:, None, :]) * grad_z...]
where the time goes in v1:
time: 30.4 us; the launch traced here: 29.9 us
  Pallas kernels  18.5 us (61%)
  local copies, waits for them, and re-layouts  10.8 us (36%)
  between operations  0.66 us (2%)
    pallas_call x1, Pallas kernels, local(): pl.pallas_call(functools.partial(kernel, n, m, scale), out_shape=(wide, w...  18.5 us
    unnamed x20, local copies, waits for them, and re-layouts  10.8 us

profile of v1, /device:TPU:0, one launch (start us, length us, event | category | flops | bytes accessed | tf_op | source)
XLA Modules:
  0.0 29.9 jit_solution(2699525306231315573)
XLA Ops:
  0.6 0.0 copy-start
  0.6 1.0 %copy-done = bf16[128,2048]{1,0:T(8,128)(2,1)S(1)} copy-done((bf16[128,2048]{1,0:T(8,128)(2,1)S(1)}, bf16[128,2048]{1,0:T(8,128)(2,1)}, u32[]{:S(2)}) %copy-start) | copy-done | bytes 524312
  1.7 0.0 copy-start.1
  1.7 1.0 %copy-done.1 = bf16[128,2048]{1,0:T(8,128)(2,1)S(1)} copy-done((bf16[128,2048]{1,0:T(8,128)(2,1)S(1)}, bf16[128,2048]{1,0:T(8,128)(2,1)}, u32[]{:S(2)}) %copy-start.1) | copy-done | bytes 524312
  2.7 0.0 copy-start.2
  2.7 1.0 %copy-done.2 = bf16[128,2048]{1,0:T(8,128)(2,1)S(1)} copy-done((bf16[128,2048]{1,0:T(8,128)(2,1)S(1)}, bf16[128,2048]{1,0:T(8,128)(2,1)}, u32[]{:S(2)}) %copy-start.2) | copy-done | bytes 524312
  3.8 0.0 copy-start.3
  3.8 1.0 %copy-done.3 = bf16[128,2048]{1,0:T(8,128)(2,1)S(1)} copy-done((bf16[128,2048]{1,0:T(8,128)(2,1)S(1)}, bf16[128,2048]{1,0:T(8,128)(2,1)}, u32[]{:S(2)}) %copy-start.3) | copy-done | bytes 524312
  4.8 0.0 copy-start.4
  4.8 0.8 %copy-done.4 = f32[4,2048]{1,0:T(4,128)S(1)} copy-done((f32[4,2048]{1,0:T(4,128)S(1)}, f32[4,2048]{1,0:T(4,128)}, u32[]{:S(2)}) %copy-start.4) | copy-done | bytes 32792
  5.6 0.0 copy-start.5
  5.6 0.8 %copy-done.5 = f32[4,2048]{1,0:T(4,128)S(1)} copy-done((f32[4,2048]{1,0:T(4,128)S(1)}, f32[4,2048]{1,0:T(4,128)}, u32[]{:S(2)}) %copy-start.5) | copy-done | bytes 32792
  6.3 0.0 copy-start.6
  6.3 0.7 %copy-done.6 = f32[2048]{0:T(1024)S(1)} copy-done((f32[2048]{0:T(1024)S(1)}, f32[2048]{0:T(1024)}, u32[]{:S(2)}) %copy-start.6) | copy-done | bytes 8216
  7.0 18.5 %hyena.1 = (bf16[128,2048]{1,0:T(8,128)(2,1)S(1)}, bf16[128,2048]{1,0:T(8,128)(2,1)S(1)}, bf16[128,2048]{1,0:T(8,128)(2,1)S(1)}, bf16[128,2048]{1,0:T(8,128)(2,1...) custom-call(bf16[128,2048]{1,0:T(8,128)(2,1)S(1)} %copy-done, bf16[128,2048]{1,0:T(8,128)(2,1)S(1)} %copy-done.1, ...), custom_call_target="tpu_custom_call" | custom-call | flops 20971520 | bytes 4194304 | tf_op jit(solution)/shard_map/hyena/pallas_call | solution.py:381
  25.5 0.8 %copy.19 = bf16[128,2048]{1,0:T(8,128)(2,1)} copy(bf16[128,2048]{1,0:T(8,128)(2,1)S(1)} %get-tuple-element.24) | data formatting | bytes 1048576
  26.3 0.8 %copy.20 = bf16[128,2048]{1,0:T(8,128)(2,1)} copy(bf16[128,2048]{1,0:T(8,128)(2,1)S(1)} %get-tuple-element.25) | data formatting | bytes 1048576
  27.1 0.8 %copy.21 = bf16[128,2048]{1,0:T(8,128)(2,1)} copy(bf16[128,2048]{1,0:T(8,128)(2,1)S(1)} %get-tuple-element.26) | data formatting | bytes 1048576
  27.9 0.8 %copy.22 = bf16[128,2048]{1,0:T(8,128)(2,1)} copy(bf16[128,2048]{1,0:T(8,128)(2,1)S(1)} %get-tuple-element.27) | data formatting | bytes 1048576
  28.7 0.6 %copy.23 = f32[4,2048]{1,0:T(4,128)} copy(f32[4,2048]{1,0:T(4,128)S(1)} %get-tuple-element.28) | data formatting | bytes 65536
  29.3 0.6 %copy.24 = f32[2048]{0:T(1024)} copy(f32[2048]{0:T(1024)S(1)} %bitcast.3) | data formatting | bytes 16384
Async XLA Ops:
  0.6 1.0 %copy-start = (bf16[128,2048]{1,0:T(8,128)(2,1)S(1)}, bf16[128,2048]{1,0:T(8,128)(2,1)}, u32[]{:S(2)}) copy-start(bf16[128,2048]{1,0:T(8,128)(2,1)} %q_hbm.1) | copy-start | bytes 1572868
  1.7 1.0 %copy-start.1 = (bf16[128,2048]{1,0:T(8,128)(2,1)S(1)}, bf16[128,2048]{1,0:T(8,128)(2,1)}, u32[]{:S(2)}) copy-start(bf16[128,2048]{1,0:T(8,128)(2,1)} %k_hbm.1) | copy-start | bytes 1572868
  2.7 1.0 %copy-start.2 = (bf16[128,2048]{1,0:T(8,128)(2,1)S(1)}, bf16[128,2048]{1,0:T(8,128)(2,1)}, u32[]{:S(2)}) copy-start(bf16[128,2048]{1,0:T(8,128)(2,1)} %v_hbm.1) | copy-start | bytes 1572868
  3.8 1.0 %copy-start.3 = (bf16[128,2048]{1,0:T(8,128)(2,1)S(1)}, bf16[128,2048]{1,0:T(8,128)(2,1)}, u32[]{:S(2)}) copy-start(bf16[128,2048]{1,0:T(8,128)(2,1)} %g_hbm.1) | copy-start | bytes 1572868
  4.8 0.8 %copy-start.4 = (f32[4,2048]{1,0:T(4,128)S(1)}, f32[4,2048]{1,0:T(4,128)}, u32[]{:S(2)}) copy-start(f32[4,2048]{1,0:T(4,128)} %decay_hbm.1) | copy-start | bytes 98308
  5.6 0.8 %copy-start.5 = (f32[4,2048]{1,0:T(4,128)S(1)}, f32[4,2048]{1,0:T(4,128)}, u32[]{:S(2)}) copy-start(f32[4,2048]{1,0:T(4,128)} %residue_hbm.1) | copy-start | bytes 98308
  6.3 0.7 %copy-start.6 = (f32[2048]{0:T(1024)S(1)}, f32[2048]{0:T(1024)}, u32[]{:S(2)}) copy-start(f32[2048]{0:T(1024)} %param.13) | copy-start | bytes 24580

commit v2 on v1

--- a/solution.py
+++ b/solution.py
@@ -40,12 +40,11 @@
 def kernel(
     n, m, scale,
     q_hbm, k_hbm, v_hbm, g_hbm, decay_hbm, residue_hbm, skip_hbm,
-    out_hbm, dq_hbm, dk_hbm, dv_hbm, res_ref, skipg_ref,
+    out_v, dq_v, dk_v, dv_v, res_ref, skipg_ref,
     q_in, k_in, v_in, g_in, decay, residue, skip, coef,
-    out_v, dq_v, dk_v, dv_v,
     x_s, z_s, y_s, u_s, seg, start,
     mine, gath, ret, carry, rsend, rgath, rtot,
-    in_sem, par_sem, out_sem, s1s, s1r, s2s, s2r, s3s, s3r, s4s, s4r,
+    in_sem, par_sem, s1s, s1r, s2s, s2r, s3s, s3r, s4s, s4r,
 ):
     me = lax.axis_index("ctx")
     rows = q_hbm.shape[0]
@@ -57,8 +56,6 @@
     own = me // stride
     hbm_in = (q_hbm, k_hbm, v_hbm, g_hbm)
     vmem_in = (q_in, k_in, v_in, g_in)
-    hbm_out = (out_hbm, dq_hbm, dk_hbm, dv_hbm)
-    vmem_out = (out_v, dq_v, dk_v, dv_v)
 
     def block_of(step):
         return lax.rem(me + 1 + step, m)
@@ -74,12 +71,6 @@
             in_sem.at[index, block],
         )
 
-    def store_copy(index, block):
-        return pltpu.make_async_copy(
-            vmem_out[index].at[block], hbm_out[index].at[:, lanes_of(block)],
-            out_sem.at[index, block],
-        )
-
     params = [
         pltpu.make_async_copy(decay_hbm, decay, par_sem.at[0]),
         pltpu.make_async_copy(residue_hbm, residue, par_sem.at[1]),
@@ -117,7 +108,10 @@
         return jnp.broadcast_to(ref[mode:mode + 1, lanes_of(block, tile)], (SEGS, LANES))
 
     def strided(index):
-        return pl.ds(index, SEGS, stride=steps)
+        return pl.ds(index, SEGS, stride=steps + 1)
+
+    def padded(first, count):
+        return pl.ds(first + first // steps, count)
 
     barrier = pltpu.get_barrier_semaphore()
     for copy in params:
@@ -136,8 +130,11 @@
         for tile in range(tiles):
             spot = block * tiles + tile
             here = slice(tile * LANES, (tile + 1) * LANES)
-            x_s[spot] = k_in[block, :, here].astype(F32) * v_in[block, :, here].astype(F32)
-            z_s[spot] = g_in[block, :, here].astype(F32) * q_in[block, :, here].astype(F32)
+            for j in range(SEGS):
+                at = slice(j * steps, (j + 1) * steps)
+                to = padded(j * steps, steps)
+                x_s[spot, to, :] = k_in[block, at, here].astype(F32) * v_in[block, at, here].astype(F32)
+                z_s[spot, to, :] = g_in[block, at, here].astype(F32) * q_in[block, at, here].astype(F32)
             d_all = decay[:, lanes_of(block, tile)]
             spread = jnp.sqrt((1.0 - d_all) * (1.0 + d_all))
             coef[:, lanes_of(block, tile)] = residue[:, lanes_of(block, tile)] * spread
@@ -284,7 +281,7 @@
             for pair in range(rows // 16):
                 parts = []
                 for half in range(2):
-                    at = slice(pair * 16 + half * 8, pair * 16 + half * 8 + 8)
+                    at = padded(pair * 16 + half * 8, 8)
                     parts.append(y_s[spot, at, :] + ((fore[0] + fore[1]) + (fore[2] + fore[3])))
                     fore = [value * rate for value, rate in zip(fore, fall)]
                 mixed = jnp.concatenate(parts, axis=0)
@@ -294,7 +291,7 @@
                 pair = rows // 16 - 1 - pair
                 parts = []
                 for half in (1, 0):
-                    at = slice(pair * 16 + half * 8, pair * 16 + half * 8 + 8)
+                    at = padded(pair * 16 + half * 8, 8)
                     parts.append(u_s[spot, at, :] + ((aft[0] + aft[1]) + (aft[2] + aft[3])))
                     aft = [value * rate for value, rate in zip(aft, fall)]
                 mixed = jnp.concatenate(parts[::-1], axis=0)
@@ -331,8 +328,6 @@
             remote(carry.at[block], carry.at[block], s2s.at[0], s2r.at[block], me).wait_recv()
 
         last_pass(block)
-        for index in range(4):
-            store_copy(index, block).start()
 
     pl.loop(0, half)(last)
     as_owner(owner_sums)
@@ -358,10 +353,24 @@
 
     as_owner(sent)
 
-    @pl.loop(0, m)
-    def _(block):
-        for index in range(4):
-            store_copy(index, block).wait()
+
+def write_kernel(m, *refs):
+    sem = refs[12]
+    width = refs[6].shape[1] // m
+    copies = []
+    for index in range(4):
+        for block in range(m):
+            copies.append(pltpu.make_async_copy(
+                refs[index].at[block],
+                refs[6 + index].at[:, block * width:(block + 1) * width],
+                sem.at[index, block],
+            ))
+    for index in range(4, 6):
+        copies.append(pltpu.make_async_copy(refs[index], refs[6 + index], sem.at[index, 0]))
+    for copy in copies:
+        copy.start()
+    for copy in copies:
+        copy.wait()
 
 
 def local(n, query, key, value, cotangent, decay, residue, skip):
@@ -371,34 +380,33 @@
     width = chans // m
     scale = 1.0 / math.sqrt(rows * n)
     wide = jax.ShapeDtypeStruct((rows, chans), jnp.bfloat16)
-    anywhere = pl.BlockSpec(memory_space=pl.ANY)
+    blocked = jax.ShapeDtypeStruct((m, rows, width), jnp.bfloat16)
+    small = (
+        jax.ShapeDtypeStruct((modes, chans), F32), jax.ShapeDtypeStruct((1, chans), F32),
+    )
+    hbm = pl.BlockSpec(memory_space=pltpu.HBM)
     vmem = pl.BlockSpec(memory_space=pltpu.VMEM)
     blocks16 = pltpu.VMEM((m, rows, width), jnp.bfloat16)
-    plane = pltpu.VMEM((chans // LANES, rows, LANES), F32)
+    plane = pltpu.VMEM((chans // LANES, rows + SEGS, LANES), F32)
     by_owner = pltpu.VMEM((m, 2 * modes, width), F32)
     by_device = pltpu.VMEM((n, 2 * modes, width), F32)
     dma = pltpu.SemaphoreType.DMA
     outs = pl.pallas_call(
         functools.partial(kernel, n, m, scale),
-        out_shape=(
-            wide, wide, wide, wide,
-            jax.ShapeDtypeStruct((modes, chans), F32),
-            jax.ShapeDtypeStruct((1, chans), F32),
-        ),
-        in_specs=[anywhere] * 7,
-        out_specs=(anywhere,) * 4 + (vmem,) * 2,
+        out_shape=(blocked,) * 4 + small,
+        in_specs=[hbm] * 7,
+        out_specs=(vmem,) * 6,
         scratch_shapes=[
             blocks16, blocks16, blocks16, blocks16,
             pltpu.VMEM((modes, chans), F32),
             pltpu.VMEM((modes, chans), F32),
             pltpu.VMEM((1, chans), F32),
             pltpu.VMEM((modes, chans), F32),
-            blocks16, blocks16, blocks16, blocks16,
             plane, plane, plane, plane,
             pltpu.VMEM((width // LANES, 2 * modes * SEGS, LANES), F32),
             pltpu.VMEM((chans // LANES, 2 * modes * SEGS, LANES), F32),
             by_owner, by_device, by_device, by_owner, by_owner, by_device, by_owner,
-            dma((4, m)), dma((3,)), dma((4, m)),
+            dma((4, m)), dma((3,)),
             dma((m,)), dma((n,)), dma((n,)), dma((m,)),
             dma((m,)), dma((n,)), dma((n,)), dma((m,)),
         ],
@@ -409,7 +417,21 @@
             flops=80 * rows * chans, bytes_accessed=16 * rows * chans, transcendentals=0
         ),
         name="hyena",
-    )(query, key, value, cotangent, decay, residue, skip.reshape(1, chans))
+    )(*[
+        pltpu.with_memory_space_constraint(array, pltpu.HBM)
+        for array in (query, key, value, cotangent, decay, residue, skip.reshape(1, chans))
+    ])
+    outs = pl.pallas_call(
+        functools.partial(write_kernel, m),
+        out_shape=(wide,) * 4 + small,
+        in_specs=[vmem] * 6,
+        out_specs=(hbm,) * 6,
+        scratch_shapes=[dma((6, m))],
+        cost_estimate=pl.CostEstimate(
+            flops=0, bytes_accessed=16 * rows * chans, transcendentals=0
+        ),
+        name="write",
+    )(*outs)
     return outs[:5] + (outs[5].reshape(chans),)
 
 

time: 30.4 us -> 25.9 us (0.85)
  local copies, waits for them, and re-layouts: 10.8 us -> 4.37 us
  Pallas kernels: 18.5 us -> 20.6 us
    unnamed x20 -> x12, local copies, waits for them, and re-layouts: 10.8 us -> 4.37 us
    pallas_call x1 -> x2, Pallas kernels: 18.5 us -> 20.6 us  [the longest x1 17.4 us: local(): pl.pallas_call(functools.partial(kernel, n, m, scale), out_shape=(blocked...]
where the time goes in v2:
time: 25.9 us; the launch traced here: 25.7 us
  Pallas kernels  20.6 us (80%)
  local copies, waits for them, and re-layouts  4.37 us (17%)
  between operations  0.66 us (3%)
    pallas_call x1, Pallas kernels, local(): pl.pallas_call(functools.partial(kernel, n, m, scale), out_shape=(blocked...  17.4 us
    unnamed x12, local copies, waits for them, and re-layouts  4.37 us
    pallas_call x1, Pallas kernels, local(): pl.pallas_call(functools.partial(write_kernel, m), out_shape=(wide,) * 4...  3.24 us

profile of v2, /device:TPU:0, one launch (start us, length us, event | category | flops | bytes accessed | tf_op | source)
XLA Modules:
  0.0 25.7 jit_solution(9705860655086055061)
XLA Ops:
  0.6 17.4 %hyena.1 = (bf16[8,128,256]{2,1,0:T(8,128)(2,1)S(1)}, bf16[8,128,256]{2,1,0:T(8,128)(2,1)S(1)}, bf16[8,128,256]{2,1,0:T(8,128)(2,1)S(1)}, bf16[8,128,256]{2,1,0:...) custom-call(bf16[128,2048]{1,0:T(8,128)(2,1)} %q_hbm.1, bf16[128,2048]{1,0:T(8,128)(2,1)} %k_hbm.1, ...), custom_call_target="tpu_custom_call" | custom-call | flops 20971520 | bytes 4194304 | tf_op jit(solution)/shard_map/hyena/pallas_call | solution.py:394
  18.0 0.0 copy-start
  18.1 0.8 %copy-done = bf16[8,128,256]{2,1,0:T(8,128)(2,1)} copy-done((bf16[8,128,256]{2,1,0:T(8,128)(2,1)}, bf16[8,128,256]{2,1,0:T(8,128)(2,1)S(1)}, u32[]{:S(2)}) %copy-start) | copy-done | bytes 524312
  18.8 0.0 copy-start.1
  18.8 0.8 %copy-done.1 = bf16[8,128,256]{2,1,0:T(8,128)(2,1)} copy-done((bf16[8,128,256]{2,1,0:T(8,128)(2,1)}, bf16[8,128,256]{2,1,0:T(8,128)(2,1)S(1)}, u32[]{:S(2)}) %copy-start.1) | copy-done | bytes 524312
  19.6 0.0 copy-start.2
  19.6 0.8 %copy-done.2 = bf16[8,128,256]{2,1,0:T(8,128)(2,1)} copy-done((bf16[8,128,256]{2,1,0:T(8,128)(2,1)}, bf16[8,128,256]{2,1,0:T(8,128)(2,1)S(1)}, u32[]{:S(2)}) %copy-start.2) | copy-done | bytes 524312
  20.4 0.0 copy-start.3
  20.4 0.8 %copy-done.3 = bf16[8,128,256]{2,1,0:T(8,128)(2,1)} copy-done((bf16[8,128,256]{2,1,0:T(8,128)(2,1)}, bf16[8,128,256]{2,1,0:T(8,128)(2,1)S(1)}, u32[]{:S(2)}) %copy-start.3) | copy-done | bytes 524312
  21.2 0.0 copy-start.4
  21.2 0.6 %copy-done.4 = f32[4,2048]{1,0:T(4,128)} copy-done((f32[4,2048]{1,0:T(4,128)}, f32[4,2048]{1,0:T(4,128)S(1)}, u32[]{:S(2)}) %copy-start.4) | copy-done | bytes 32792
  21.8 0.0 copy-start.5
  21.8 0.6 %copy-done.5 = f32[1,2048]{1,0:T(1,128)} copy-done((f32[1,2048]{1,0:T(1,128)}, f32[1,2048]{1,0:T(1,128)S(1)}, u32[]{:S(2)}) %copy-start.5) | copy-done | bytes 8216
  22.4 3.2 %write.1 = (bf16[128,2048]{1,0:T(8,128)(2,1)}, bf16[128,2048]{1,0:T(8,128)(2,1)}, bf16[128,2048]{1,0:T(8,128)(2,1)}, bf16[128,2048]{1,0:T(8,128)(2,1)}, f32[4,2048]{1,0:T(4,128)}, /*index=5*/f32[1,2048]{1,0:T(1,128)}) custom-call(bf16[8,128,256]{2,1,0:T(8,128)(2,1)} %copy-done, bf16[8,128,256]{2,1,0:T(8,128)(2,1)} %copy-done.1, ...), custom_call_target="tpu_custom_call" | custom-call | bytes 4194304 | tf_op jit(solution)/shard_map/write/pallas_call | solution.py:424
Async XLA Ops:
  18.0 0.8 %copy-start = (bf16[8,128,256]{2,1,0:T(8,128)(2,1)}, bf16[8,128,256]{2,1,0:T(8,128)(2,1)S(1)}, u32[]{:S(2)}) copy-start(bf16[8,128,256]{2,1,0:T(8,128)(2,1)S(1)} %get-tuple-element.18.refs_0_) | copy-start | bytes 1572868
  18.8 0.8 %copy-start.1 = (bf16[8,128,256]{2,1,0:T(8,128)(2,1)}, bf16[8,128,256]{2,1,0:T(8,128)(2,1)S(1)}, u32[]{:S(2)}) copy-start(bf16[8,128,256]{2,1,0:T(8,128)(2,1)S(1)} %get-tuple-element.19.refs_1_) | copy-start | bytes 1572868
  19.6 0.8 %copy-start.2 = (bf16[8,128,256]{2,1,0:T(8,128)(2,1)}, bf16[8,128,256]{2,1,0:T(8,128)(2,1)S(1)}, u32[]{:S(2)}) copy-start(bf16[8,128,256]{2,1,0:T(8,128)(2,1)S(1)} %get-tuple-element.20.refs_2_) | copy-start | bytes 1572868
  20.4 0.8 %copy-start.3 = (bf16[8,128,256]{2,1,0:T(8,128)(2,1)}, bf16[8,128,256]{2,1,0:T(8,128)(2,1)S(1)}, u32[]{:S(2)}) copy-start(bf16[8,128,256]{2,1,0:T(8,128)(2,1)S(1)} %get-tuple-element.21.refs_3_) | copy-start | bytes 1572868
  21.2 0.6 %copy-start.4 = (f32[4,2048]{1,0:T(4,128)}, f32[4,2048]{1,0:T(4,128)S(1)}, u32[]{:S(2)}) copy-start(f32[4,2048]{1,0:T(4,128)S(1)} %get-tuple-element.22.refs_4_) | copy-start | bytes 98308
  21.8 0.6 %copy-start.5 = (f32[1,2048]{1,0:T(1,128)}, f32[1,2048]{1,0:T(1,128)S(1)}, u32[]{:S(2)}) copy-start(f32[1,2048]{1,0:T(1,128)S(1)} %get-tuple-element.23.refs_5_) | copy-start | bytes 24580

commit v3 on v2

--- a/solution.py
+++ b/solution.py
@@ -40,9 +40,8 @@
 def kernel(
     n, m, scale,
     q_hbm, k_hbm, v_hbm, g_hbm, decay_hbm, residue_hbm, skip_hbm,
-    out_v, dq_v, dk_v, dv_v, res_ref, skipg_ref,
-    q_in, k_in, v_in, g_in, decay, residue, skip, coef,
-    x_s, z_s, y_s, u_s, seg, start,
+    q_in, k_in, v_in, g_in, y_s, u_s, decay, coef, carried, res_ref, skipg_ref,
+    residue, skip, x_s, z_s, seg, start,
     mine, gath, ret, carry, rsend, rgath, rtot,
     in_sem, par_sem, s1s, s1r, s2s, s2r, s3s, s3r, s4s, s4r,
 ):
@@ -127,6 +126,7 @@
     def first_pass(block):
         for index in range(4):
             load_copy(index, block).wait()
+        d = []
         for tile in range(tiles):
             spot = block * tiles + tile
             here = slice(tile * LANES, (tile + 1) * LANES)
@@ -135,34 +135,39 @@
                 to = padded(j * steps, steps)
                 x_s[spot, to, :] = k_in[block, at, here].astype(F32) * v_in[block, at, here].astype(F32)
                 z_s[spot, to, :] = g_in[block, at, here].astype(F32) * q_in[block, at, here].astype(F32)
+            d.append([row(decay, mode, block, tile) for mode in range(modes)])
+        tail = [[None] * modes for _ in range(tiles)]
+        head = [[None] * modes for _ in range(tiles)]
+        for i in range(steps):
+            for tile in range(tiles):
+                spot = block * tiles + tile
+                x = x_s[spot, strided(i), :]
+                z = z_s[spot, strided(steps - 1 - i), :]
+                for mode in range(modes):
+                    tail[tile][mode] = x if i == 0 else d[tile][mode] * tail[tile][mode] + x
+                    head[tile][mode] = z if i == 0 else d[tile][mode] * head[tile][mode] + z
+        for tile in range(tiles):
+            for mode in range(modes):
+                seg[tile, mode * SEGS:(mode + 1) * SEGS, :] = tail[tile][mode]
+                seg[tile, (modes + mode) * SEGS:(modes + mode + 1) * SEGS, :] = head[tile][mode]
+        for tile in range(tiles):
+            spot = block * tiles + tile
+            here = slice(tile * LANES, (tile + 1) * LANES)
             d_all = decay[:, lanes_of(block, tile)]
             spread = jnp.sqrt((1.0 - d_all) * (1.0 + d_all))
             coef[:, lanes_of(block, tile)] = residue[:, lanes_of(block, tile)] * spread
-            d = [row(decay, mode, block, tile) for mode in range(modes)]
-            tail = [None] * modes
-            head = [None] * modes
-            for i in range(steps):
-                x = x_s[spot, strided(i), :]
-                z = z_s[spot, strided(steps - 1 - i), :]
-                for mode in range(modes):
-                    tail[mode] = x if i == 0 else d[mode] * tail[mode] + x
-                    head[mode] = z if i == 0 else d[mode] * head[mode] + z
-            for mode in range(modes):
-                seg[tile, mode * SEGS:(mode + 1) * SEGS, :] = tail[mode]
-                seg[tile, (modes + mode) * SEGS:(modes + mode + 1) * SEGS, :] = head[mode]
             d_seg = power(d_all, steps)
-            total = jnp.zeros((modes, LANES), F32)
+            up = jnp.zeros((modes, LANES), F32)
+            down = jnp.zeros((modes, LANES), F32)
             for j in range(SEGS):
                 at = pl.ds(j, modes, stride=SEGS)
-                start[spot, at, :] = total
-                total = d_seg * total + seg[tile, at, :]
-            mine[block, 0:modes, here] = total
-            total = jnp.zeros((modes, LANES), F32)
-            for j in reversed(range(SEGS)):
-                at = pl.ds(modes * SEGS + j, modes, stride=SEGS)
-                start[spot, at, :] = total
-                total = d_seg * total + seg[tile, at, :]
-            mine[block, modes:2 * modes, here] = total
+                start[spot, at, :] = up
+                up = d_seg * up + seg[tile, at, :]
+                at = pl.ds(modes * SEGS + SEGS - 1 - j, modes, stride=SEGS)
+                start[spot, at, :] = down
+                down = d_seg * down + seg[tile, at, :]
+            mine[block, 0:modes, here] = up
+            mine[block, modes:2 * modes, here] = down
 
     def send_ends(block):
         @pl.when(block * stride != me)
@@ -173,38 +178,60 @@
         def _():
             gath[me] = mine[block]
 
-    def middle_pass(block):
-        for tile in range(tiles):
-            spot = block * tiles + tile
-            here = slice(tile * LANES, (tile + 1) * LANES)
-            d = [row(decay, mode, block, tile) for mode in range(modes)]
-            c = [row(coef, mode, block, tile) for mode in range(modes)]
-            sk = row(skip, 0, block, tile)
-            state = [start[spot, mode * SEGS:(mode + 1) * SEGS, :] for mode in range(modes)]
-            back = [
-                start[spot, (modes + mode) * SEGS:(modes + mode + 1) * SEGS, :]
+    def rows_of(ref, block, count):
+        return [[row(ref, mode, block, tile) for mode in range(count)] for tile in range(tiles)]
+
+    def states_of(first, block):
+        return [
+            [
+                start[block * tiles + tile, (first + mode) * SEGS:(first + mode + 1) * SEGS, :]
                 for mode in range(modes)
             ]
-            sums = [jnp.zeros((SEGS, LANES), F32) for _ in range(modes + 1)]
-            for i in range(steps):
+            for tile in range(tiles)
+        ]
+
+    def forward_pass(block):
+        d = rows_of(decay, block, modes)
+        c = rows_of(coef, block, modes)
+        sk = rows_of(skip, block, 1)
+        state = states_of(0, block)
+        sums = [[None] * (modes + 1) for _ in range(tiles)]
+        for i in range(steps):
+            for tile in range(tiles):
+                spot = block * tiles + tile
                 x = x_s[spot, strided(i), :]
                 z = z_s[spot, strided(i), :]
-                y = sk * x
-                sums[modes] = sums[modes] + z * x
+                y = sk[tile][0] * x
+                terms = []
                 for mode in range(modes):
-                    state[mode] = d[mode] * state[mode] + x
-                    y = y + c[mode] * state[mode]
-                    sums[mode] = sums[mode] + z * state[mode]
+                    now = d[tile][mode] * state[tile][mode] + x
+                    state[tile][mode] = now
+                    y = y + c[tile][mode] * now
+                    terms.append(z * now)
+                terms.append(z * x)
+                sums[tile] = terms if i == 0 else [a + b for a, b in zip(sums[tile], terms)]
                 y_s[spot, strided(i), :] = y
-                z = z_s[spot, strided(steps - 1 - i), :]
-                u = sk * z
+        for tile in range(tiles):
+            here = slice(tile * LANES, (tile + 1) * LANES)
+            for mode in range(modes + 1):
+                rsend[block, mode:mode + 1, here] = jnp.sum(sums[tile][mode], axis=0, keepdims=True)
+            rsend[block, modes + 1:, here] = jnp.zeros((modes - 1, LANES), F32)
+
+    def backward_pass(block):
+        d = rows_of(decay, block, modes)
+        c = rows_of(coef, block, modes)
+        sk = rows_of(skip, block, 1)
+        back = states_of(modes, block)
+        for i in reversed(range(steps)):
+            for tile in range(tiles):
+                spot = block * tiles + tile
+                z = z_s[spot, strided(i), :]
+                u = sk[tile][0] * z
                 for mode in range(modes):
-                    back[mode] = d[mode] * back[mode] + z
-                    u = u + c[mode] * back[mode]
-                u_s[spot, strided(steps - 1 - i), :] = u
-            for mode in range(modes + 1):
-                rsend[block, mode:mode + 1, here] = jnp.sum(sums[mode], axis=0, keepdims=True)
-            rsend[block, modes + 1:, here] = jnp.zeros((2 * modes - modes - 1, LANES), F32)
+                    now = d[tile][mode] * back[tile][mode] + z
+                    back[tile][mode] = now
+                    u = u + c[tile][mode] * now
+                u_s[spot, strided(i), :] = u
 
     def send_sums(block):
         @pl.when(block * stride != me)
@@ -255,6 +282,94 @@
         rtot[own, modes:2 * modes, :] = whole[modes:2 * modes] * scale
         peers(lambda peer: total_copy(peer).start())
 
+    first_pass(block_of(0))
+    pl.semaphore_wait(barrier, n - 1)
+    send_ends(block_of(0))
+
+    @pl.loop(1, m)
+    def _(step):
+        block = block_of(step)
+        first_pass(block)
+        send_ends(block)
+
+    @pl.loop(0, m)
+    def _(step):
+        block = block_of(step)
+        forward_pass(block)
+        send_sums(block)
+
+    as_owner(owner_scan)
+    late = m - m // 4
+
+    @pl.loop(0, late)
+    def _(step):
+        backward_pass(block_of(step))
+
+    as_owner(owner_sums)
+
+    @pl.loop(late, m)
+    def _(step):
+        backward_pass(block_of(step))
+
+    for block in range(m):
+        @pl.when(block * stride != me)
+        def _():
+            remote(carry.at[block], carry.at[block], s2s.at[0], s2r.at[block], me).wait_recv()
+            remote(rtot.at[block], rtot.at[block], s4s.at[0], s4r.at[block], me).wait_recv()
+            ends_copy(block).wait_send()
+            sums_copy(block).wait_send()
+
+        at = slice(block * width, (block + 1) * width)
+        res_ref[:, at] = rtot[block, 0:modes, :]
+        skipg_ref[:, at] = rtot[block, modes:modes + 1, :]
+        carried[block] = carry[block]
+
+    def sent():
+        def one(peer):
+            return_copy(peer).wait_send()
+            total_copy(peer).wait_send()
+
+        peers(one)
+
+    as_owner(sent)
+
+
+def last_kernel(
+    m,
+    q_in, k_in, v_in, g_in, y_s, u_s, decay, coef, carried, res_ref, skipg_ref,
+    out_hbm, dq_hbm, dk_hbm, dv_hbm, res_hbm, skipg_hbm,
+    out_v, dq_v, dk_v, dv_v, out_sem, small_sem,
+):
+    rows, width = q_in.shape[1:]
+    tiles = width // LANES
+    modes = decay.shape[0]
+    steps = rows // SEGS
+    hbm_out = (out_hbm, dq_hbm, dk_hbm, dv_hbm)
+    vmem_out = (out_v, dq_v, dk_v, dv_v)
+
+    def lanes_of(block, tile):
+        return pl.ds(pl.multiple_of(block * width + tile * LANES, LANES), LANES)
+
+    def row(ref, mode, block, tile):
+        return jnp.broadcast_to(ref[mode:mode + 1, lanes_of(block, tile)], (SEGS, LANES))
+
+    def padded(first, count):
+        return pl.ds(first + first // steps, count)
+
+    def store_copy(index, block):
+        return pltpu.make_async_copy(
+            vmem_out[index].at[block],
+            hbm_out[index].at[:, pl.ds(pl.multiple_of(block * width, LANES), width)],
+            out_sem.at[index, block],
+        )
+
+    small = [
+        pltpu.make_async_copy(res_ref, res_hbm, small_sem.at[0]),
+        pltpu.make_async_copy(skipg_ref, skipg_hbm, small_sem.at[1]),
+    ]
+    for copy in small:
+        copy.start()
+
     place = lax.broadcasted_iota(jnp.int32, (SEGS, LANES), 0)
     bits = [(place & (1 << bit)) != 0 for bit in range(3)]
 
@@ -268,9 +383,9 @@
             for mode in range(modes):
                 base = row(decay, mode, block, tile)
                 weight = row(coef, mode, block, tile) * base
-                up = weight * jnp.broadcast_to(carry[block, mode:mode + 1, here], (SEGS, LANES))
+                up = weight * jnp.broadcast_to(carried[block, mode:mode + 1, here], (SEGS, LANES))
                 down = weight * jnp.broadcast_to(
-                    carry[block, modes + mode:modes + mode + 1, here], (SEGS, LANES))
+                    carried[block, modes + mode:modes + mode + 1, here], (SEGS, LANES))
                 for bit in bits:
                     up = jnp.where(bit, up * base, up)
                     down = jnp.where(bit, down, down * base)
@@ -299,78 +414,19 @@
                 dk_v[block, at, here] = (v_in[block, at, here].astype(F32) * mixed).astype(jnp.bfloat16)
                 dv_v[block, at, here] = (k_in[block, at, here].astype(F32) * mixed).astype(jnp.bfloat16)
 
-    first_pass(block_of(0))
-    pl.semaphore_wait(barrier, n - 1)
-    send_ends(block_of(0))
-
-    @pl.loop(1, m)
-    def _(step):
-        block = block_of(step)
-        first_pass(block)
-        send_ends(block)
-
-    half = m // 2
-
-    def middle(step):
-        block = block_of(step)
-        middle_pass(block)
-        send_sums(block)
-
-    pl.loop(0, half)(middle)
-    as_owner(owner_scan)
-    pl.loop(half, m)(middle)
-
-    def last(step):
-        block = block_of(m - 1 + step)
-
-        @pl.when(block * stride != me)
-        def _():
-            remote(carry.at[block], carry.at[block], s2s.at[0], s2r.at[block], me).wait_recv()
-
+    @pl.loop(0, m)
+    def _(block):
         last_pass(block)
-
-    pl.loop(0, half)(last)
-    as_owner(owner_sums)
-    pl.loop(half, m)(last)
-
-    for block in range(m):
-        @pl.when(block * stride != me)
-        def _():
-            remote(rtot.at[block], rtot.at[block], s4s.at[0], s4r.at[block], me).wait_recv()
-            ends_copy(block).wait_send()
-            sums_copy(block).wait_send()
-
-        at = slice(block * width, (block + 1) * width)
-        res_ref[:, at] = rtot[block, 0:modes, :]
-        skipg_ref[:, at] = rtot[block, modes:modes + 1, :]
-
-    def sent():
-        def one(peer):
-            return_copy(peer).wait_send()
-            total_copy(peer).wait_send()
-
-        peers(one)
-
-    as_owner(sent)
-
-
-def write_kernel(m, *refs):
-    sem = refs[12]
-    width = refs[6].shape[1] // m
-    copies = []
-    for index in range(4):
-        for block in range(m):
-            copies.append(pltpu.make_async_copy(
-                refs[index].at[block],
-                refs[6 + index].at[:, block * width:(block + 1) * width],
-                sem.at[index, block],
-            ))
-    for index in range(4, 6):
-        copies.append(pltpu.make_async_copy(refs[index], refs[6 + index], sem.at[index, 0]))
-    for copy in copies:
-        copy.start()
-    for copy in copies:
+        for index in range(4):
+            store_copy(index, block).start()
+
+    for copy in small:
         copy.wait()
+
+    @pl.loop(0, m)
+    def _(block):
+        for index in range(4):
+            store_copy(index, block).wait()
 
 
 def local(n, query, key, value, cotangent, decay, residue, skip):
@@ -380,7 +436,6 @@
     width = chans // m
     scale = 1.0 / math.sqrt(rows * n)
     wide = jax.ShapeDtypeStruct((rows, chans), jnp.bfloat16)
-    blocked = jax.ShapeDtypeStruct((m, rows, width), jnp.bfloat16)
     small = (
         jax.ShapeDtypeStruct((modes, chans), F32), jax.ShapeDtypeStruct((1, chans), F32),
     )
@@ -388,21 +443,21 @@
     vmem = pl.BlockSpec(memory_space=pltpu.VMEM)
     blocks16 = pltpu.VMEM((m, rows, width), jnp.bfloat16)
     plane = pltpu.VMEM((chans // LANES, rows + SEGS, LANES), F32)
+    per_mode = pltpu.VMEM((modes, chans), F32)
+    per_chan = pltpu.VMEM((1, chans), F32)
     by_owner = pltpu.VMEM((m, 2 * modes, width), F32)
     by_device = pltpu.VMEM((n, 2 * modes, width), F32)
     dma = pltpu.SemaphoreType.DMA
-    outs = pl.pallas_call(
+    held = pl.pallas_call(
         functools.partial(kernel, n, m, scale),
-        out_shape=(blocked,) * 4 + small,
+        out_shape=(
+            blocks16, blocks16, blocks16, blocks16, plane, plane,
+            per_mode, per_mode, by_owner, per_mode, per_chan,
+        ),
         in_specs=[hbm] * 7,
-        out_specs=(vmem,) * 6,
+        out_specs=(vmem,) * 11,
         scratch_shapes=[
-            blocks16, blocks16, blocks16, blocks16,
-            pltpu.VMEM((modes, chans), F32),
-            pltpu.VMEM((modes, chans), F32),
-            pltpu.VMEM((1, chans), F32),
-            pltpu.VMEM((modes, chans), F32),
-            plane, plane, plane, plane,
+            per_mode, per_chan, plane, plane,
             pltpu.VMEM((width // LANES, 2 * modes * SEGS, LANES), F32),
             pltpu.VMEM((chans // LANES, 2 * modes * SEGS, LANES), F32),
             by_owner, by_device, by_device, by_owner, by_owner, by_device, by_owner,
@@ -411,27 +466,28 @@
             dma((m,)), dma((n,)), dma((n,)), dma((m,)),
         ],
         compiler_params=pltpu.CompilerParams(
-            collective_id=0, has_side_effects=True, vmem_limit_bytes=20 * 1024 * 1024,
+            collective_id=0, has_side_effects=True, vmem_limit_bytes=24 * 1024 * 1024,
         ),
         cost_estimate=pl.CostEstimate(
-            flops=80 * rows * chans, bytes_accessed=16 * rows * chans, transcendentals=0
+            flops=60 * rows * chans, bytes_accessed=8 * rows * chans, transcendentals=0
         ),
-        name="hyena",
+        name="states",
     )(*[
         pltpu.with_memory_space_constraint(array, pltpu.HBM)
         for array in (query, key, value, cotangent, decay, residue, skip.reshape(1, chans))
     ])
     outs = pl.pallas_call(
-        functools.partial(write_kernel, m),
+        functools.partial(last_kernel, m),
         out_shape=(wide,) * 4 + small,
-        in_specs=[vmem] * 6,
+        in_specs=[vmem] * 11,
         out_specs=(hbm,) * 6,
-        scratch_shapes=[dma((6, m))],
+        scratch_shapes=[blocks16] * 4 + [dma((4, m)), dma((2,))],
+        compiler_params=pltpu.CompilerParams(vmem_limit_bytes=24 * 1024 * 1024),
         cost_estimate=pl.CostEstimate(
-            flops=0, bytes_accessed=16 * rows * chans, transcendentals=0
+            flops=30 * rows * chans, bytes_accessed=8 * rows * chans, transcendentals=0
         ),
-        name="write",
-    )(*outs)
+        name="gates",
+    )(*[pltpu.with_memory_space_constraint(array, pltpu.VMEM) for array in held])
     return outs[:5] + (outs[5].reshape(chans),)
 
 

time: 25.9 us -> 18 us (0.69)
  local copies, waits for them, and re-layouts: 4.37 us -> 0 us
  Pallas kernels: 20.6 us -> 17.2 us
    unnamed x12 -> x0, local copies, waits for them, and re-layouts: 4.37 us -> none
    pallas_call x2, Pallas kernels: 20.6 us -> 17.2 us  [the longest x1 15.1 us: local(): pl.pallas_call(functools.partial(kernel, n, m, scale), out_shape=(blocks1...]
where the time goes in v3:
time: 18 us; the launch traced here: 17.8 us
  Pallas kernels  17.2 us (96%)
  between operations  0.64 us (4%)
    pallas_call x1, Pallas kernels, local(): pl.pallas_call(functools.partial(kernel, n, m, scale), out_shape=(blocks1...  15.1 us
    pallas_call x1, Pallas kernels, local(): pl.pallas_call(functools.partial(last_kernel, m), out_shape=(wide,) * 4 +...  2.12 us

profile of v3, /device:TPU:0, one launch (start us, length us, event | category | flops | bytes accessed | tf_op | source)
XLA Modules:
  0.0 17.8 jit_solution(7321036539316815629)
XLA Ops:
  0.6 15.1 %states.1 = (bf16[8,128,256]{2,1,0:T(8,128)(2,1)S(1)}, bf16[8,128,256]{2,1,0:T(8,128)(2,1)S(1)}, bf16[8,128,256]{2,1,0:T(8,128)(2,1)S(1)}, bf16[8,128,256]{2,1,0...) custom-call(bf16[128,2048]{1,0:T(8,128)(2,1)} %q_hbm.1, ...), custom_call_target="tpu_custom_call" | custom-call | flops 15728640 | bytes 2097152 | tf_op jit(solution)/shard_map/states/pallas_call | solution.py:451
  15.7 2.1 %gates.1 = (bf16[128,2048]{1,0:T(8,128)(2,1)}, bf16[128,2048]{1,0:T(8,128)(2,1)}, bf16[128,2048]{1,0:T(8,128)(2,1)}, bf16[128,2048]{1,0:T(8,128)(2,1)}, f32[4,2048]{1,0:T(4,128)}, /*index=5*/f32[1,2048]{1,0:T(1,128)}) custom-call(bf16[8,128,256]{2,1,0:T(8,128)(2,1)S(1)} %get-tuple-element.23.q_in, bf16[8,128,256]{2,1,0:T(8,128)(2,1)S(1)} %get-tuple-element.24.k_in, ...), custom_call_target="tpu_custom_call" | custom-call | flops 7864320 | bytes 2097152 | tf_op jit(solution)/shard_map/gates/pallas_call | solution.py:479

commit v4 on v3

--- a/solution.py
+++ b/solution.py
@@ -40,10 +40,9 @@
 def kernel(
     n, m, scale,
     q_hbm, k_hbm, v_hbm, g_hbm, decay_hbm, residue_hbm, skip_hbm,
-    q_in, k_in, v_in, g_in, y_s, u_s, decay, coef, carried, res_ref, skipg_ref,
-    residue, skip, x_s, z_s, seg, start,
-    mine, gath, ret, carry, rsend, rgath, rtot,
-    in_sem, par_sem, s1s, s1r, s2s, s2r, s3s, s3r, s4s, s4r,
+    q_in, k_in, v_in, g_in, y_s, u_s, decay, coef, carry,
+    residue, skip, x_s, z_s, seg, start, mine, gath, ret,
+    in_sem, par_sem, s1s, s1r, s2s, s2r,
 ):
     me = lax.axis_index("ctx")
     rows = q_hbm.shape[0]
@@ -87,12 +86,6 @@
 
     def return_copy(peer):
         return remote(ret.at[peer], carry.at[own], s2s.at[peer], s2r.at[own], peer)
-
-    def sums_copy(block):
-        return remote(rsend.at[block], rgath.at[me], s3s.at[block], s3r.at[me], block * stride)
-
-    def total_copy(peer):
-        return remote(rtot.at[own], rtot.at[own], s4s.at[peer], s4r.at[own], peer)
 
     def as_owner(body):
         if stride == 1:
@@ -138,14 +131,18 @@
             d.append([row(decay, mode, block, tile) for mode in range(modes)])
         tail = [[None] * modes for _ in range(tiles)]
         head = [[None] * modes for _ in range(tiles)]
+        sums = [None] * tiles
         for i in range(steps):
             for tile in range(tiles):
                 spot = block * tiles + tile
                 x = x_s[spot, strided(i), :]
                 z = z_s[spot, strided(steps - 1 - i), :]
+                beside = z_s[spot, strided(i), :]
                 for mode in range(modes):
                     tail[tile][mode] = x if i == 0 else d[tile][mode] * tail[tile][mode] + x
                     head[tile][mode] = z if i == 0 else d[tile][mode] * head[tile][mode] + z
+                terms = [beside * now for now in tail[tile] + [x]]
+                sums[tile] = terms if i == 0 else [a + b for a, b in zip(sums[tile], terms)]
         for tile in range(tiles):
             for mode in range(modes):
                 seg[tile, mode * SEGS:(mode + 1) * SEGS, :] = tail[tile][mode]
@@ -168,6 +165,14 @@
                 down = d_seg * down + seg[tile, at, :]
             mine[block, 0:modes, here] = up
             mine[block, modes:2 * modes, here] = down
+            for mode in range(modes + 1):
+                total = sums[tile][mode]
+                if mode < modes:
+                    begun = start[spot, mode * SEGS:(mode + 1) * SEGS, :]
+                    total = total + d[tile][mode] * head[tile][mode] * begun
+                at = 2 * modes + mode
+                mine[block, at:at + 1, here] = jnp.sum(total, axis=0, keepdims=True)
+            mine[block, 3 * modes + 1:, here] = jnp.zeros((modes - 1, LANES), F32)
 
     def send_ends(block):
         @pl.when(block * stride != me)
@@ -190,57 +195,26 @@
             for tile in range(tiles)
         ]
 
-    def forward_pass(block):
+    def middle_pass(block):
         d = rows_of(decay, block, modes)
         c = rows_of(coef, block, modes)
         sk = rows_of(skip, block, 1)
         state = states_of(0, block)
-        sums = [[None] * (modes + 1) for _ in range(tiles)]
+        back = states_of(modes, block)
         for i in range(steps):
             for tile in range(tiles):
                 spot = block * tiles + tile
                 x = x_s[spot, strided(i), :]
-                z = z_s[spot, strided(i), :]
+                z = z_s[spot, strided(steps - 1 - i), :]
                 y = sk[tile][0] * x
-                terms = []
-                for mode in range(modes):
-                    now = d[tile][mode] * state[tile][mode] + x
-                    state[tile][mode] = now
-                    y = y + c[tile][mode] * now
-                    terms.append(z * now)
-                terms.append(z * x)
-                sums[tile] = terms if i == 0 else [a + b for a, b in zip(sums[tile], terms)]
-                y_s[spot, strided(i), :] = y
-        for tile in range(tiles):
-            here = slice(tile * LANES, (tile + 1) * LANES)
-            for mode in range(modes + 1):
-                rsend[block, mode:mode + 1, here] = jnp.sum(sums[tile][mode], axis=0, keepdims=True)
-            rsend[block, modes + 1:, here] = jnp.zeros((modes - 1, LANES), F32)
-
-    def backward_pass(block):
-        d = rows_of(decay, block, modes)
-        c = rows_of(coef, block, modes)
-        sk = rows_of(skip, block, 1)
-        back = states_of(modes, block)
-        for i in reversed(range(steps)):
-            for tile in range(tiles):
-                spot = block * tiles + tile
-                z = z_s[spot, strided(i), :]
                 u = sk[tile][0] * z
                 for mode in range(modes):
-                    now = d[tile][mode] * back[tile][mode] + z
-                    back[tile][mode] = now
-                    u = u + c[tile][mode] * now
-                u_s[spot, strided(i), :] = u
-
-    def send_sums(block):
-        @pl.when(block * stride != me)
-        def _():
-            sums_copy(block).start()
-
-        @pl.when(block * stride == me)
-        def _():
-            rgath[me] = rsend[block]
+                    state[tile][mode] = d[tile][mode] * state[tile][mode] + x
+                    back[tile][mode] = d[tile][mode] * back[tile][mode] + z
+                    y = y + c[tile][mode] * state[tile][mode]
+                    u = u + c[tile][mode] * back[tile][mode]
+                y_s[spot, strided(i), :] = y
+                u_s[spot, strided(steps - 1 - i), :] = u
 
     def owner_scan():
         peers(lambda peer: remote(
@@ -258,29 +232,27 @@
         zero = jnp.zeros((modes, width), F32)
         lax.fori_loop(0, n, forward, zero, unroll=n <= 16)
         lax.fori_loop(0, n, backward, zero, unroll=n <= 16)
+
+        def add(p, total):
+            return (
+                total[0] + gath[p, 2 * modes:, :],
+                total[1] + gath[p, modes:2 * modes, :] * ret[p, 0:modes, :],
+            )
+
+        whole, cross = lax.fori_loop(
+            0, n, add, (jnp.zeros((2 * modes, width), F32), zero), unroll=n <= 16)
+        d_all = decay[:, lanes_of(own)]
+        spread = jnp.sqrt((1.0 - d_all) * (1.0 + d_all))
+        weights = (whole[0:modes] + d_all * cross) * (spread * scale)
+        skips = whole[modes:] * scale
+
+        def put(p):
+            ret[p, 2 * modes:3 * modes, :] = weights
+            ret[p, 3 * modes:, :] = skips
+
+        each(0, n, put)
         carry[own] = ret[me]
         peers(lambda peer: return_copy(peer).start())
-
-    def owner_sums():
-        peers(lambda peer: remote(
-            rgath.at[peer], rgath.at[peer], s3s.at[0], s3r.at[peer], peer).wait_recv())
-
-        def add(p, total):
-            return (
-                total[0] + rgath[p],
-                total[1] + gath[p, modes:2 * modes, :] * ret[p, 0:modes, :],
-            )
-
-        whole, cross = lax.fori_loop(
-            0, n, add,
-            (jnp.zeros((2 * modes, width), F32), jnp.zeros((modes, width), F32)),
-            unroll=n <= 16,
-        )
-        d_all = decay[:, lanes_of(own)]
-        spread = jnp.sqrt((1.0 - d_all) * (1.0 + d_all))
-        rtot[own, 0:modes, :] = (whole[0:modes] + d_all * cross) * (spread * scale)
-        rtot[own, modes:2 * modes, :] = whole[modes:2 * modes] * scale
-        peers(lambda peer: total_copy(peer).start())
 
     first_pass(block_of(0))
     pl.semaphore_wait(barrier, n - 1)
@@ -292,53 +264,32 @@
         first_pass(block)
         send_ends(block)
 
-    @pl.loop(0, m)
+    half = m // 2
+
+    @pl.loop(0, half)
     def _(step):
-        block = block_of(step)
-        forward_pass(block)
-        send_sums(block)
+        middle_pass(block_of(step))
 
     as_owner(owner_scan)
-    late = m - m // 4
-
-    @pl.loop(0, late)
+
+    @pl.loop(half, m)
     def _(step):
-        backward_pass(block_of(step))
-
-    as_owner(owner_sums)
-
-    @pl.loop(late, m)
-    def _(step):
-        backward_pass(block_of(step))
+        middle_pass(block_of(step))
 
     for block in range(m):
         @pl.when(block * stride != me)
         def _():
+            ends_copy(block).wait_send()
             remote(carry.at[block], carry.at[block], s2s.at[0], s2r.at[block], me).wait_recv()
-            remote(rtot.at[block], rtot.at[block], s4s.at[0], s4r.at[block], me).wait_recv()
-            ends_copy(block).wait_send()
-            sums_copy(block).wait_send()
-
-        at = slice(block * width, (block + 1) * width)
-        res_ref[:, at] = rtot[block, 0:modes, :]
-        skipg_ref[:, at] = rtot[block, modes:modes + 1, :]
-        carried[block] = carry[block]
-
-    def sent():
-        def one(peer):
-            return_copy(peer).wait_send()
-            total_copy(peer).wait_send()
-
-        peers(one)
-
-    as_owner(sent)
+
+    as_owner(lambda: peers(lambda peer: return_copy(peer).wait_send()))
 
 
 def last_kernel(
     m,
-    q_in, k_in, v_in, g_in, y_s, u_s, decay, coef, carried, res_ref, skipg_ref,
+    q_in, k_in, v_in, g_in, y_s, u_s, decay, coef, carried,
     out_hbm, dq_hbm, dk_hbm, dv_hbm, res_hbm, skipg_hbm,
-    out_v, dq_v, dk_v, dv_v, out_sem, small_sem,
+    out_v, dq_v, dk_v, dv_v, res_ref, skipg_ref, out_sem, small_sem,
 ):
     rows, width = q_in.shape[1:]
     tiles = width // LANES
@@ -363,6 +314,10 @@
             out_sem.at[index, block],
         )
 
+    for block in range(m):
+        at = slice(block * width, (block + 1) * width)
+        res_ref[:, at] = carried[block, 2 * modes:3 * modes, :]
+        skipg_ref[:, at] = carried[block, 3 * modes:3 * modes + 1, :]
     small = [
         pltpu.make_async_copy(res_ref, res_hbm, small_sem.at[0]),
         pltpu.make_async_copy(skipg_ref, skipg_hbm, small_sem.at[1]),
@@ -445,24 +400,23 @@
     plane = pltpu.VMEM((chans // LANES, rows + SEGS, LANES), F32)
     per_mode = pltpu.VMEM((modes, chans), F32)
     per_chan = pltpu.VMEM((1, chans), F32)
-    by_owner = pltpu.VMEM((m, 2 * modes, width), F32)
-    by_device = pltpu.VMEM((n, 2 * modes, width), F32)
+    by_owner = pltpu.VMEM((m, 4 * modes, width), F32)
+    by_device = pltpu.VMEM((n, 4 * modes, width), F32)
     dma = pltpu.SemaphoreType.DMA
     held = pl.pallas_call(
         functools.partial(kernel, n, m, scale),
         out_shape=(
             blocks16, blocks16, blocks16, blocks16, plane, plane,
-            per_mode, per_mode, by_owner, per_mode, per_chan,
+            per_mode, per_mode, by_owner,
         ),
         in_specs=[hbm] * 7,
-        out_specs=(vmem,) * 11,
+        out_specs=(vmem,) * 9,
         scratch_shapes=[
             per_mode, per_chan, plane, plane,
             pltpu.VMEM((width // LANES, 2 * modes * SEGS, LANES), F32),
             pltpu.VMEM((chans // LANES, 2 * modes * SEGS, LANES), F32),
-            by_owner, by_device, by_device, by_owner, by_owner, by_device, by_owner,
+            by_owner, by_device, by_device,
             dma((4, m)), dma((3,)),
-            dma((m,)), dma((n,)), dma((n,)), dma((m,)),
             dma((m,)), dma((n,)), dma((n,)), dma((m,)),
         ],
         compiler_params=pltpu.CompilerParams(
@@ -479,9 +433,9 @@
     outs = pl.pallas_call(
         functools.partial(last_kernel, m),
         out_shape=(wide,) * 4 + small,
-        in_specs=[vmem] * 11,
+        in_specs=[vmem] * 9,
         out_specs=(hbm,) * 6,
-        scratch_shapes=[blocks16] * 4 + [dma((4, m)), dma((2,))],
+        scratch_shapes=[blocks16] * 4 + [per_mode, per_chan, dma((4, m)), dma((2,))],
         compiler_params=pltpu.CompilerParams(vmem_limit_bytes=24 * 1024 * 1024),
         cost_estimate=pl.CostEstimate(
             flops=30 * rows * chans, bytes_accessed=8 * rows * chans, transcendentals=0

time: 18 us -> 17.5 us (0.972)
  Pallas kernels: 17.2 us -> 16.7 us
    pallas_call x1, Pallas kernels: 15.1 us -> 14.6 us  [local(): pl.pallas_call(functools.partial(kernel, n, m, scale), out_shape=(blocks1...]
where the time goes in v4:
time: 17.5 us; the launch traced here: 17.3 us
  Pallas kernels  16.7 us (95%)
  between operations  0.64 us (4%)
    pallas_call x1, Pallas kernels, local(): pl.pallas_call(functools.partial(kernel, n, m, scale), out_shape=(blocks1...  14.6 us
    pallas_call x1, Pallas kernels, local(): pl.pallas_call(functools.partial(last_kernel, m), out_shape=(wide,) * 4 +...  2.14 us

profile of v4, /device:TPU:0, one launch (start us, length us, event | category | flops | bytes accessed | tf_op | source)
XLA Modules:
  0.0 17.3 jit_solution(5603674402420520213)
XLA Ops:
  0.6 14.6 %states.1 = (bf16[8,128,256]{2,1,0:T(8,128)(2,1)S(1)}, bf16[8,128,256]{2,1,0:T(8,128)(2,1)S(1)}, bf16[8,128,256]{2,1,0:T(8,128)(2,1)S(1)}, bf16[8,128,256]{2,1,0...) custom-call(bf16[128,2048]{1,0:T(8,128)(2,1)} %q_hbm.1, ...), custom_call_target="tpu_custom_call" | custom-call | flops 15728640 | bytes 2097152 | tf_op jit(solution)/shard_map/states/pallas_call | solution.py:406
  15.2 2.1 %gates.1 = (bf16[128,2048]{1,0:T(8,128)(2,1)}, bf16[128,2048]{1,0:T(8,128)(2,1)}, bf16[128,2048]{1,0:T(8,128)(2,1)}, bf16[128,2048]{1,0:T(8,128)(2,1)}, f32[4,2048]{1,0:T(4,128)}, /*index=5*/f32[1,2048]{1,0:T(1,128)}) custom-call(bf16[8,128,256]{2,1,0:T(8,128)(2,1)S(1)} %get-tuple-element.21.q_in, bf16[8,128,256]{2,1,0:T(8,128)(2,1)S(1)} %get-tuple-element.22.k_in, ...), custom_call_target="tpu_custom_call" | custom-call | flops 7864320 | bytes 2097152 | tf_op jit(solution)/shard_map/gates/pallas_call | solution.py:433

commit v5 on v4

--- a/solution.py
+++ b/solution.py
@@ -24,6 +24,14 @@
             return carry
 
         lax.fori_loop(low, high, wrapped, 0)
+
+
+def far_first(index, size, step):
+    if size % 2:
+        return lax.rem(index + 1 + step, size)
+    half = size // 2
+    later = step // half
+    return lax.rem(index // half + 1 + later, 2) * half + lax.rem(index + step + later, half)
 
 
 def power(base, exponent):
@@ -56,7 +64,7 @@
     vmem_in = (q_in, k_in, v_in, g_in)
 
     def block_of(step):
-        return lax.rem(me + 1 + step, m)
+        return far_first(own, m, step)
 
     def lanes_of(block, tile=None):
         if tile is None:
@@ -94,7 +102,7 @@
             pl.when(lax.rem(me, stride) == 0)(body)
 
     def peers(body):
-        each(1, n, lambda r: body(lax.rem(me + r, n)))
+        each(0, n - 1, lambda step: body(far_first(me, n, step)))
 
     def row(ref, mode, block, tile):
         return jnp.broadcast_to(ref[mode:mode + 1, lanes_of(block, tile)], (SEGS, LANES))
@@ -106,13 +114,13 @@
         return pl.ds(first + first // steps, count)
 
     barrier = pltpu.get_barrier_semaphore()
+    peers(lambda peer: pl.semaphore_signal(
+        barrier, inc=1, device_id={"ctx": peer}, device_id_type=MESH))
     for copy in params:
         copy.start()
     for step in range(m):
         for index in range(4):
             load_copy(index, block_of(step)).start()
-    peers(lambda peer: pl.semaphore_signal(
-        barrier, inc=1, device_id={"ctx": peer}, device_id_type=MESH))
     for copy in params:
         copy.wait()
 

time: 17.5 us -> 17.7 us (1.011)
  Pallas kernels: 16.7 us -> 16.9 us
where the time goes in v5:
time: 17.7 us; the launch traced here: 17.5 us
  Pallas kernels  16.9 us (95%)
  between operations  0.64 us (4%)
    pallas_call x1, Pallas kernels, local(): pl.pallas_call(functools.partial(kernel, n, m, scale), out_shape=(blocks1...  14.7 us
    pallas_call x1, Pallas kernels, local(): pl.pallas_call(functools.partial(last_kernel, m), out_shape=(wide,) * 4 +...  2.14 us

profile of v5, /device:TPU:0, one launch (start us, length us, event | category | flops | bytes accessed | tf_op | source)
XLA Modules:
  0.0 17.5 jit_solution(16224661736368257049)
XLA Ops:
  0.6 14.7 %states.1 = (bf16[8,128,256]{2,1,0:T(8,128)(2,1)S(1)}, bf16[8,128,256]{2,1,0:T(8,128)(2,1)S(1)}, bf16[8,128,256]{2,1,0:T(8,128)(2,1)S(1)}, bf16[8,128,256]{2,1,0...) custom-call(bf16[128,2048]{1,0:T(8,128)(2,1)} %q_hbm.1, ...), custom_call_target="tpu_custom_call" | custom-call | flops 15728640 | bytes 2097152 | tf_op jit(solution)/shard_map/states/pallas_call | solution.py:414
  15.4 2.1 %gates.1 = (bf16[128,2048]{1,0:T(8,128)(2,1)}, bf16[128,2048]{1,0:T(8,128)(2,1)}, bf16[128,2048]{1,0:T(8,128)(2,1)}, bf16[128,2048]{1,0:T(8,128)(2,1)}, f32[4,2048]{1,0:T(4,128)}, /*index=5*/f32[1,2048]{1,0:T(1,128)}) custom-call(bf16[8,128,256]{2,1,0:T(8,128)(2,1)S(1)} %get-tuple-element.21.q_in, bf16[8,128,256]{2,1,0:T(8,128)(2,1)S(1)} %get-tuple-element.22.k_in, ...), custom_call_target="tpu_custom_call" | custom-call | flops 7864320 | bytes 2097152 | tf_op jit(solution)/shard_map/gates/pallas_call | solution.py:441
